TPU v7x, 32 devices: a whole 2x2x4 slice. The times are simulated.
32 devices in a mesh: rec: 8 (over z, y), src: 4 (over x, core).
Axes of the slice: x: 2, y: 2, z: 4, core: 2. Of those that a mesh axis runs over, the one named last changes fastest.
Arguments:
- kernel: float32 [2, 2, 5120, 5120], P(None, None, 'rec', 'src'), may hold values from -0.0625 to 0.0625
- traces: float32 [4, 2560, 2, 2, 256], P('src', 'rec')
- acq_lists: int32 [4, 2560], P('src', 'rec'), may hold values from 0 to 1279, as said below
- counts: int32 [4, 8], P('src', 'rec'), may hold values from 1 to 320, as said below
Outputs:
- solution: float32 [5120, 2, 2, 256], P(('src', 'rec'))
- next_left: float32 [5120, 2, 2, 256], P(('rec', 'src'))
Inputs may be any that keep to these rules, and one draw needn't show every extreme that they name: `acq_lists`: an id a * 160 + k names row k of area a. Within each list the first counts[s, r] slots of the blocks name every id exactly once; other slots hold ids to be ignored. No block names more than 40 ids of one area, and every block that names an area names exactly 40 of its ids. `counts`: used slots of a block; in every list some block uses all 320.
All inputs are finite; a program needn't handle non-finite values.
Results may differ from a plain program's by a relative error of at most 0.00026.
Values sent between devices are 32-bit elements; how exact they have to be, the bound alone decides.
No kernel may reach another device: no remote copies, remote signals or barrier semaphores. Data moves between devices by JAX's collectives and lax.ppermute only.
A program may use at most 128 MiB of HBM per device.

v0:
```python
import jax
import jax.numpy as jnp
from jax import lax
from jax.sharding import PartitionSpec as P

NR = 5120
FREQS = 2
SOURCES = 256
ITERS = 2


def kernel_apply(kernel, vector):
    highest = lax.Precision.HIGHEST
    real_part = jnp.einsum("fmc,cfn->mfn", kernel[0], vector[:, 0], precision=highest) - jnp.einsum(
        "fmc,cfn->mfn", kernel[1], vector[:, 1], precision=highest
    )
    imag_part = jnp.einsum("fmc,cfn->mfn", kernel[0], vector[:, 1], precision=highest) + jnp.einsum(
        "fmc,cfn->mfn", kernel[1], vector[:, 0], precision=highest
    )
    return jnp.stack([real_part, imag_part], axis=1)


def kernel_adjoint(kernel, vector):
    highest = lax.Precision.HIGHEST
    real_part = jnp.einsum("fmc,mfn->cfn", kernel[0], vector[:, 0], precision=highest) + jnp.einsum(
        "fmc,mfn->cfn", kernel[1], vector[:, 1], precision=highest
    )
    imag_part = jnp.einsum("fmc,mfn->cfn", kernel[0], vector[:, 1], precision=highest) - jnp.einsum(
        "fmc,mfn->cfn", kernel[1], vector[:, 0], precision=highest
    )
    return jnp.stack([real_part, imag_part], axis=1)


def widen(values):
    return values[None, None, :, None]


def rms_norm(vector):
    local_sum = jnp.sum(vector * vector, axis=(0, 1, 3))
    global_sum = lax.psum(local_sum, ("rec", "src"))
    return jnp.sqrt(global_sum / (2.0 * NR * SOURCES))


def on_device(kernel, traces, acq_lists, counts):
    highest = lax.Precision.HIGHEST
    my_area = lax.axis_index("rec")
    row_count = kernel.shape[2] // lax.axis_size("src")
    slot_count = traces.shape[1]
    width = traces.shape[2] * traces.shape[3] * traces.shape[4]
    row_iota = jnp.arange(row_count, dtype=jnp.int32)
    piece_traces = lax.all_gather(traces, "rec", axis=1, tiled=True)
    piece_ids = lax.all_gather(acq_lists, "rec", axis=1, tiled=True)
    piece_counts = lax.all_gather(counts, "rec", axis=1, tiled=True)
    span_slots = piece_ids.shape[1]
    slot_iota = jnp.arange(span_slots, dtype=jnp.int32)
    block_iota = jnp.arange(piece_counts.shape[1], dtype=jnp.int32)
    in_block = (slot_iota // slot_count)[:, None] == block_iota[None, :]
    limits = jnp.sum(jnp.where(in_block, piece_counts[0][None, :], 0), axis=1)
    filled = slot_iota % slot_count < limits
    list_ids = piece_ids[0]
    wanted = filled & (list_ids // row_count == my_area)
    selector = ((list_ids % row_count)[None, :] == row_iota[:, None]) & wanted[None, :]
    observed = jnp.dot(
        selector.astype(jnp.float32), piece_traces.reshape(span_slots, width), precision=highest
    )
    observed = observed.reshape(row_count, 2, FREQS, SOURCES)

    def adjoint(vector):
        spread = lax.all_gather(vector, "src", axis=0, tiled=True)
        return lax.psum_scatter(
            kernel_adjoint(kernel, spread), "rec", scatter_dimension=0, tiled=True
        )

    beta_norm = rms_norm(observed)
    left_unit = observed / widen(beta_norm)
    right_vec = adjoint(left_unit)
    alpha_norm = rms_norm(right_vec)
    right_unit = right_vec / widen(alpha_norm)
    search = right_unit
    solution = jnp.zeros(right_unit.shape, jnp.float32)
    phibar = beta_norm
    rhobar = alpha_norm
    next_left = observed
    for iteration in range(ITERS):
        forward_spread = lax.all_gather(right_unit, "rec", axis=0, tiled=True)
        next_left = (
            lax.psum_scatter(
                kernel_apply(kernel, forward_spread), "src", scatter_dimension=0, tiled=True
            )
            - widen(alpha_norm) * left_unit
        )
        beta_norm = rms_norm(next_left)
        left_unit = next_left / widen(beta_norm)
        rho_value = jnp.sqrt(rhobar * rhobar + beta_norm * beta_norm)
        cosine = rhobar / rho_value
        sine_value = beta_norm / rho_value
        phi_value = cosine * phibar
        phibar = sine_value * phibar
        solution = solution + widen(phi_value / rho_value) * search
        if iteration + 1 < ITERS:
            right_vec = adjoint(left_unit) - widen(beta_norm) * right_unit
            alpha_norm = rms_norm(right_vec)
            right_unit = right_vec / widen(alpha_norm)
            theta_value = sine_value * alpha_norm
            rhobar = -cosine * alpha_norm
            search = right_unit - widen(theta_value / rho_value) * search
    return (solution, next_left)


def solution(mesh):
    placed = (
        P(None, None, "rec", "src"),
        P("src", "rec", None, None, None),
        P("src", "rec"),
        P("src", "rec"),
    )
    return jax.shard_map(
        on_device,
        mesh=mesh,
        in_specs=placed,
        out_specs=(P(("src", "rec"), None, None, None), P(("rec", "src"), None, None, None)),
        check_vma=False,
    )
```

profile of v0, /device:TPU:0, one launch (start us, length us, event | category | flops | bytes accessed | tf_op | source)
XLA Modules:
  0.0 1079.2 jit_solution(17460557952361835040)
XLA Ops:
  7.2 0.0 all-gather.6.cloned.1.call-start
  7.2 0.7 all-gather.6.cloned.1.call-update
  7.9 0.0 all-gather.8.cloned.1.call-start
  8.6 0.7 reduce
  9.3 1.2 dynamic-slice
  11.2 0.3 dynamic-update-slice
  11.5 0.7 bitcast_dynamic-update-slice_fusion
  12.2 40.1 %all-reduce.2 = (s32[2560]{0:T(1024)S(1)}, s32[8]{0:T(128)S(1)}) all-reduce(s32[2560]{0:T(1024)S(1)} %dynamic-update-slice, s32[8]{0:T(128)S(1)} %bitcast_dynamic-update-slice_fusion), channel_id=1, replica_groups=mesh['rec'=8,'src'=4] {'rec'}, use_global_device_ids=true, to_apply=%add | all-reduce | flops 2568 | bytes 20544
  52.3 0.1 select_reduce_fusion
  52.4 0.1 and_reduce_fusion
  52.5 111.5 %all-gather.6.cloned.1.call-done = f32[1,2560,2,2,256]{4,3,2,0,1:T(2,128)} async-done(((f32[1,320,2,2,256]{4,3,2,0,1:T(2,128)}), f32[1,2560,2,2,256]{4,3,2,0,1:T(2,128)}) %all-gather.6.cloned.1.call-update) | async-done | bytes 10485776 | tf_op jit(solution)/shard_map/all_gather | solution.py:51
  164.1 16.2 %copy.146 = f32[1,2560,2,2,256]{1,4,3,2,0:T(8,128)} copy(f32[1,2560,2,2,256]{4,3,2,0,1:T(2,128)} %all-gather.6.cloned.1.call-done) | data formatting | bytes 20971520 | tf_op jit(solution)/shard_map/reshape | solution.py:64
  180.3 9.2 multiply_reduce_fusion.4
  189.5 38.4 %psum.35 = f32[2]{0:T(128)S(1)} all-reduce(f32[2]{0:T(128)S(1)} %get-tuple-element.20), channel_id=1, replica_groups=mesh['rec'=8,'src'=4] {'rec','src'}, use_global_device_ids=true, to_apply=%region_2.3 | all-reduce | flops 2 | bytes 16 | tf_op jit(solution)/shard_map/psum | solution.py:40
  227.9 1.0 broadcast_divide_fusion.3
  228.9 0.3 reduce-scatter.5.cloned.1.call-start
  229.2 26.2 %all-gather.8.cloned.1.call-done = f32[640,2,2,256]{3,0,2,1:T(8,128)} async-done(((f32[160,2,2,256]{3,0,2,1:T(8,128)}), f32[640,2,2,256]{3,0,2,1:T(8,128)}) %all-gather.8.cloned.1.call-update) | async-done | bytes 2621456 | tf_op jit(solution)/shard_map/all_gather | solution.py:69
  255.4 12.9 %fusion.14 = f32[2,256,1280]{1,2,0:T(8,128)S(1)} fusion(f32[2,2,640,1280]{3,2,1,0:T(8,128)} %param.4, f32[640,2,2,256]{3,0,2,1:T(8,128)} %all-gather.8.cloned.1.call-done), kind=kOutput, calls=%fused_computation.14 | convolution fusion | flops 5033164800 | bytes 10485760 | tf_op jit(solution)/shard_map/fmc,mfn->cfn/dot_general | solution.py:28
  268.3 12.9 %fusion.16 = f32[2,256,1280]{1,2,0:T(8,128)S(1)} fusion(f32[2,2,640,1280]{3,2,1,0:T(8,128)} %param.4, f32[640,2,2,256]{3,0,2,1:T(8,128)} %all-gather.8.cloned.1.call-done), kind=kOutput, calls=%fused_computation.16 | convolution fusion | flops 5033164800 | bytes 10485760 | tf_op jit(solution)/shard_map/fmc,mfn->cfn/dot_general | solution.py:25
  281.3 13.1 %fusion.68 = f32[1280,1,2,256]{3,0,2,1:T(8,128)S(1)} fusion(f32[2,256,1280]{1,2,0:T(8,128)S(1)} %fusion.14, f32[2,2,640,1280]{3,2,1,0:T(8,128)} %param.4, f32[640,2,2,256]{3,0,2,1:T(8,128)S(1)} %copy-done.3), kind=kOutput, calls=%fused_computation.58 | convolution fusion | flops 5033820160 | bytes 13107200 | tf_op jit(solution)/shard_map/fmc,mfn->cfn/dot_general | solution.py:28
  294.4 10.4 fusion.71
  304.9 2.8 pad_maximum_fusion
  307.6 0.0 all-gather.10.cloned.1.call-start
  307.7 102.9 %reduce-scatter.5.cloned.1.call-done = f32[160,2,2,256]{3,0,2,1:T(8,128)} async-done(((f32[1280,2,2,256]{3,0,2,1:T(8,128)}), f32[160,2,2,256]{3,0,2,1:T(8,128)}) %reduce-scatter.5.cloned.1.call-update) | async-done | bytes 655376 | tf_op jit(solution)/shard_map/reduce_scatter | solution.py:70
  410.6 1.3 multiply_reduce_fusion.3
  411.8 40.1 %psum.36 = f32[2]{0:T(128)S(1)} all-reduce(f32[2]{0:T(128)S(1)} %multiply_reduce_fusion.3), channel_id=1, replica_groups=mesh['rec'=8,'src'=4] {'rec','src'}, use_global_device_ids=true, to_apply=%region_5.6 | all-reduce | flops 2 | bytes 16 | tf_op jit(solution)/shard_map/psum | solution.py:40
  452.0 2.1 broadcast_divide_fusion.2
  454.1 0.0 reduce-scatter.7.cloned.1.call-start
  454.1 86.0 %all-gather.10.cloned.1.call-done = f32[1280,2,2,256]{3,0,2,1:T(8,128)} async-done(((f32[160,2,2,256]{3,0,2,1:T(8,128)}), f32[1280,2,2,256]{3,0,2,1:T(8,128)}) %all-gather.10.cloned.1.call-update) | async-done | bytes 5242896 | tf_op jit(solution)/shard_map/all_gather | solution.py:85
  540.1 9.4 fusion.10
  549.5 9.2 fusion.12
  558.8 7.8 fusion.86
  566.6 5.9 fusion.80
  572.6 1.7 pad_maximum_fusion.2
  574.3 0.0 all-gather.12.cloned.1.call-start
  574.3 32.9 %reduce-scatter.7.cloned.1.call-done = f32[160,2,2,256]{3,0,2,1:T(8,128)} async-done(((f32[640,2,2,256]{3,0,2,1:T(8,128)}), f32[160,2,2,256]{3,0,2,1:T(8,128)}) %reduce-scatter.7.cloned.1.call-update) | async-done | bytes 655376 | tf_op jit(solution)/shard_map/reduce_scatter | solution.py:87
  607.2 1.4 multiply_reduce_fusion.2
  608.6 39.3 %psum.37 = f32[2]{0:T(128)S(1)} all-reduce(f32[2]{0:T(128)S(1)} %multiply_reduce_fusion.2), channel_id=1, replica_groups=mesh['rec'=8,'src'=4] {'rec','src'}, use_global_device_ids=true, to_apply=%region_8.9 | all-reduce | flops 2 | bytes 16 | tf_op jit(solution)/shard_map/psum | solution.py:40
  647.9 2.1 broadcast_divide_fusion.1
  650.1 0.0 reduce-scatter.9.cloned.1.call-start
  650.1 26.4 %all-gather.12.cloned.1.call-done = f32[640,2,2,256]{3,0,2,1:T(8,128)} async-done(((f32[160,2,2,256]{3,0,2,1:T(8,128)}), f32[640,2,2,256]{3,0,2,1:T(8,128)}) %all-gather.12.cloned.1.call-update) | async-done | bytes 2621456 | tf_op jit(solution)/shard_map/all_gather | solution.py:69
  676.5 13.4 %fusion.6 = f32[2,256,1280]{1,2,0:T(8,128)S(1)} fusion(f32[2,2,640,1280]{3,2,1,0:T(8,128)} %param.4, f32[640,2,2,256]{3,0,2,1:T(8,128)} %all-gather.12.cloned.1.call-done), kind=kOutput, calls=%fused_computation.6 | convolution fusion | flops 5033164800 | bytes 10485760 | tf_op jit(solution)/shard_map/fmc,mfn->cfn/dot_general | solution.py:28
  689.9 12.9 %fusion.8 = f32[2,256,1280]{1,2,0:T(8,128)S(1)} fusion(f32[2,2,640,1280]{3,2,1,0:T(8,128)} %param.4, f32[640,2,2,256]{3,0,2,1:T(8,128)} %all-gather.12.cloned.1.call-done), kind=kOutput, calls=%fused_computation.8 | convolution fusion | flops 5033164800 | bytes 10485760 | tf_op jit(solution)/shard_map/fmc,mfn->cfn/dot_general | solution.py:25
  702.9 12.8 %fusion.62 = f32[1280,1,2,256]{3,0,2,1:T(8,128)S(1)} fusion(f32[2,256,1280]{1,2,0:T(8,128)S(1)} %fusion.6, f32[2,2,640,1280]{3,2,1,0:T(8,128)} %param.4, f32[640,2,2,256]{3,0,2,1:T(8,128)S(1)} %copy-done.4), kind=kOutput, calls=%fused_computation.56 | convolution fusion | flops 5033820160 | bytes 13107200 | tf_op jit(solution)/shard_map/fmc,mfn->cfn/dot_general | solution.py:28
  715.7 10.4 fusion.65
  726.1 2.8 pad_maximum_fusion.1
  728.9 0.0 all-gather.14.cloned.1.call-start
  729.0 102.7 %reduce-scatter.9.cloned.1.call-done = f32[160,2,2,256]{3,0,2,1:T(8,128)} async-done(((f32[1280,2,2,256]{3,0,2,1:T(8,128)}), f32[160,2,2,256]{3,0,2,1:T(8,128)}) %reduce-scatter.9.cloned.1.call-update) | async-done | bytes 655376 | tf_op jit(solution)/shard_map/reduce_scatter | solution.py:70
  831.7 1.4 multiply_reduce_fusion.1
  833.0 40.3 %psum.38 = f32[2]{0:T(128)S(1)} all-reduce(f32[2]{0:T(128)S(1)} %multiply_reduce_fusion.1), channel_id=1, replica_groups=mesh['rec'=8,'src'=4] {'rec','src'}, use_global_device_ids=true, to_apply=%region_11.12 | all-reduce | flops 2 | bytes 16 | tf_op jit(solution)/shard_map/psum | solution.py:40
  873.4 2.1 broadcast_divide_fusion
  875.5 0.0 reduce-scatter.11.cloned.1.call-start
  875.6 86.0 %all-gather.14.cloned.1.call-done = f32[1280,2,2,256]{3,0,2,1:T(8,128)} async-done(((f32[160,2,2,256]{3,0,2,1:T(8,128)}), f32[1280,2,2,256]{3,0,2,1:T(8,128)}) %all-gather.14.cloned.1.call-update) | async-done | bytes 5242896 | tf_op jit(solution)/shard_map/all_gather | solution.py:85
  961.6 9.2 fusion.2
  970.8 9.2 fusion.4
  980.1 7.8 fusion.98
  988.0 5.9 fusion.92
  993.9 1.7 pad_maximum_fusion.3
  995.6 33.0 %reduce-scatter.11.cloned.1.call-done = f32[160,2,2,256]{3,0,2,1:T(8,128)} async-done(((f32[640,2,2,256]{3,0,2,1:T(8,128)}), f32[160,2,2,256]{3,0,2,1:T(8,128)}) %reduce-scatter.11.cloned.1.call-update) | async-done | bytes 655376 | tf_op jit(solution)/shard_map/reduce_scatter | solution.py:87
  1028.6 1.4 multiply_reduce_fusion
  1030.0 39.3 %psum.39 = f32[2]{0:T(128)S(1)} all-reduce(f32[2]{0:T(128)S(1)} %get-tuple-element.15), channel_id=1, replica_groups=mesh['rec'=8,'src'=4] {'rec','src'}, use_global_device_ids=true, to_apply=%region_14.15 | all-reduce | flops 2 | bytes 16 | tf_op jit(solution)/shard_map/psum | solution.py:40
  1069.3 0.2 multiply_add_fusion
  1069.5 1.3 copy.111
  1070.9 1.3 copy.112
  (70 shorter events, 0.4 us)
Async XLA Ops:
  7.2 156.9 %all-gather.6.cloned.1.call-start = ((), (), s32[]{:S(2)}) async-start(), calls=%async_computation.4 | async-start | bytes 11796480 | tf_op jit(solution)/shard_map/all_gather | solution.py:51
  7.9 247.5 %all-gather.8.cloned.1.call-start = ((), (), s32[]{:S(2)}) async-start(), calls=%async_computation.5 | async-start | bytes 3276800 | tf_op jit(solution)/shard_map/all_gather | solution.py:69
  228.9 181.6 %reduce-scatter.5.cloned.1.call-start = ((), (), s32[]{:S(2)}) async-start(), calls=%async_computation.6 | async-start | bytes 5898240 | tf_op jit(solution)/shard_map/reduce_scatter | solution.py:70
  255.4 39.0 %slice-start = ((s8[13107200]{0:T(1024)(128)(4,1)}), s8[4194304]{0:T(1024)(128)(4,1)S(1)}, s32[]{:S(2)}) async-start(s8[13107200]{0:T(1024)(128)(4,1)} %bitcast.167), calls=%async_computation.13 | async-start | bytes 8388608
  255.4 39.0 %slice-start.1 = ((s8[13107200]{0:T(1024)(128)(4,1)}), s8[4194304]{0:T(1024)(128)(4,1)S(1)}, s32[]{:S(2)}) async-start(s8[13107200]{0:T(1024)(128)(4,1)} %bitcast.167), calls=%async_computation.14 | async-start | bytes 8388608
  268.3 13.0 %copy-start.3 = (f32[640,2,2,256]{3,0,2,1:T(8,128)S(1)}, f32[640,2,2,256]{3,0,2,1:T(8,128)}, u32[]{:S(2)}) copy-start(f32[640,2,2,256]{3,0,2,1:T(8,128)} %all-gather.8.cloned.1.call-done) | copy-start | bytes 7864324
  268.3 26.1 %slice-start.2 = ((s8[13107200]{0:T(1024)(128)(4,1)}), s8[4194304]{0:T(1024)(128)(4,1)S(1)}, s32[]{:S(2)}) async-start(s8[13107200]{0:T(1024)(128)(4,1)} %bitcast.167), calls=%async_computation.15 | async-start | bytes 8388608
  281.3 13.1 %slice-start.3 = ((s8[13107200]{0:T(1024)(128)(4,1)}), s8[524288]{0:T(1024)(128)(4,1)S(1)}, s32[]{:S(2)}) async-start(s8[13107200]{0:T(1024)(128)(4,1)} %bitcast.167), calls=%async_computation.16 | async-start | bytes 1048576
  307.6 232.5 %all-gather.10.cloned.1.call-start = ((), (), s32[]{:S(2)}) async-start(), calls=%async_computation.7 | async-start | bytes 5898240 | tf_op jit(solution)/shard_map/all_gather | solution.py:85
  454.1 153.2 %reduce-scatter.7.cloned.1.call-start = ((), (), s32[]{:S(2)}) async-start(), calls=%async_computation.8 | async-start | bytes 3276800 | tf_op jit(solution)/shard_map/reduce_scatter | solution.py:87
  540.1 26.5 %slice-start.4 = ((s8[13107200]{0:T(1024)(128)(4,1)}), s8[4194304]{0:T(1024)(128)(4,1)S(1)}, s32[]{:S(2)}) async-start(s8[13107200]{0:T(1024)(128)(4,1)} %bitcast.169), calls=%async_computation.17 | async-start | bytes 8388608
  540.1 26.5 %slice-start.5 = ((s8[13107200]{0:T(1024)(128)(4,1)}), s8[4194304]{0:T(1024)(128)(4,1)S(1)}, s32[]{:S(2)}) async-start(s8[13107200]{0:T(1024)(128)(4,1)} %bitcast.169), calls=%async_computation.18 | async-start | bytes 8388608
  549.5 9.3 copy-start
  549.5 17.1 %slice-start.6 = ((s8[13107200]{0:T(1024)(128)(4,1)}), s8[4194304]{0:T(1024)(128)(4,1)S(1)}, s32[]{:S(2)}) async-start(s8[13107200]{0:T(1024)(128)(4,1)} %bitcast.169), calls=%async_computation.19 | async-start | bytes 8388608
  558.8 7.8 slice-start.7
  574.3 102.3 %all-gather.12.cloned.1.call-start = ((), (), s32[]{:S(2)}) async-start(), calls=%async_computation.9 | async-start | bytes 3276800 | tf_op jit(solution)/shard_map/all_gather | solution.py:69
  650.1 181.6 %reduce-scatter.9.cloned.1.call-start = ((), (), s32[]{:S(2)}) async-start(), calls=%async_computation.10 | async-start | bytes 5898240 | tf_op jit(solution)/shard_map/reduce_scatter | solution.py:70
  676.5 39.1 %slice-start.8 = ((s8[13107200]{0:T(1024)(128)(4,1)}), s8[4194304]{0:T(1024)(128)(4,1)S(1)}, s32[]{:S(2)}) async-start(s8[13107200]{0:T(1024)(128)(4,1)} %bitcast.171), calls=%async_computation.21 | async-start | bytes 8388608
  676.5 39.2 %slice-start.9 = ((s8[13107200]{0:T(1024)(128)(4,1)}), s8[4194304]{0:T(1024)(128)(4,1)S(1)}, s32[]{:S(2)}) async-start(s8[13107200]{0:T(1024)(128)(4,1)} %bitcast.171), calls=%async_computation.22 | async-start | bytes 8388608
  689.9 13.0 %copy-start.4 = (f32[640,2,2,256]{3,0,2,1:T(8,128)S(1)}, f32[640,2,2,256]{3,0,2,1:T(8,128)}, u32[]{:S(2)}) copy-start(f32[640,2,2,256]{3,0,2,1:T(8,128)} %all-gather.12.cloned.1.call-done) | copy-start | bytes 7864324
  689.9 25.8 %slice-start.10 = ((s8[13107200]{0:T(1024)(128)(4,1)}), s8[4194304]{0:T(1024)(128)(4,1)S(1)}, s32[]{:S(2)}) async-start(s8[13107200]{0:T(1024)(128)(4,1)} %bitcast.171), calls=%async_computation.23 | async-start | bytes 8388608
  702.9 12.8 %slice-start.11 = ((s8[13107200]{0:T(1024)(128)(4,1)}), s8[524288]{0:T(1024)(128)(4,1)S(1)}, s32[]{:S(2)}) async-start(s8[13107200]{0:T(1024)(128)(4,1)} %bitcast.171), calls=%async_computation.24 | async-start | bytes 1048576
  728.9 102.7 %copy-start.2 = (f32[160,2,2,256]{3,0,2,1:T(8,128)S(1)}, f32[160,2,2,256]{3,0,2,1:T(8,128)}, u32[]{:S(2)}) copy-start(f32[160,2,2,256]{3,0,2,1:T(8,128)} %reduce-scatter.5.cloned.1.call-done) | copy-start | bytes 1966084
  728.9 232.6 %all-gather.14.cloned.1.call-start = ((), (), s32[]{:S(2)}) async-start(), calls=%async_computation.11 | async-start | bytes 5898240 | tf_op jit(solution)/shard_map/all_gather | solution.py:85
  875.5 153.1 %reduce-scatter.11.cloned.1.call-start = ((), (), s32[]{:S(2)}) async-start(), calls=%async_computation.12 | async-start | bytes 3276800 | tf_op jit(solution)/shard_map/reduce_scatter | solution.py:87
  961.6 26.3 %slice-start.12 = ((s8[13107200]{0:T(1024)(128)(4,1)}), s8[4194304]{0:T(1024)(128)(4,1)S(1)}, s32[]{:S(2)}) async-start(s8[13107200]{0:T(1024)(128)(4,1)} %bitcast.173), calls=%async_computation.25 | async-start | bytes 8388608
  961.6 26.3 %slice-start.13 = ((s8[13107200]{0:T(1024)(128)(4,1)}), s8[4194304]{0:T(1024)(128)(4,1)S(1)}, s32[]{:S(2)}) async-start(s8[13107200]{0:T(1024)(128)(4,1)} %bitcast.173), calls=%async_computation.26 | async-start | bytes 8388608
  970.8 9.3 copy-start.1
  970.8 17.1 %slice-start.14 = ((s8[13107200]{0:T(1024)(128)(4,1)}), s8[4194304]{0:T(1024)(128)(4,1)S(1)}, s32[]{:S(2)}) async-start(s8[13107200]{0:T(1024)(128)(4,1)} %bitcast.173), calls=%async_computation.27 | async-start | bytes 8388608
  980.1 7.9 slice-start.15
  995.6 33.0 %copy-start.5 = (f32[160,2,2,256]{3,0,2,1:T(8,128)S(1)}, f32[160,2,2,256]{3,0,2,1:T(8,128)}, u32[]{:S(2)}) copy-start(f32[160,2,2,256]{3,0,2,1:T(8,128)} %broadcast_divide_fusion.1) | copy-start | bytes 1966084
  995.6 73.7 %copy-start.6 = (f32[160,2,2,256]{3,0,2,1:T(8,128)S(1)}, f32[160,2,2,256]{3,0,2,1:T(8,128)}, u32[]{:S(2)}) copy-start(f32[160,2,2,256]{3,0,2,1:T(8,128)} %broadcast_divide_fusion) | copy-start | bytes 1966084
Sparse Core Ops, SparseCore 0:
  10.2 153.8 all-gather.5
  229.0 26.2 all-gather.7
  307.8 102.7 reduce-scatter.4
  454.2 85.8 all-gather.9
  574.4 32.8 reduce-scatter.6
  650.2 26.2 all-gather.11
  729.1 102.5 reduce-scatter.8
  875.6 85.8 all-gather.13
  995.7 32.8 reduce-scatter.10
where the time goes:
time: 1080 us
  waiting for transfers between devices  608 us (56%)
  blocking collectives  238 us (22%)
  matrix products  173 us (16%)
  other arithmetic  22.7 us (2%)
  local copies, waits for them, and re-layouts  21.3 us (2%)
  between operations  16.1 us (1%)
    reduce_scatter x2, waiting for transfers between devices, adjoint(): lax.psum_scatter(kernel_adjoint(kernel, spread), 'rec', scatter_dimension...  206 us
    psum x5, blocking collectives, rms_norm(): global_sum = lax.psum(local_sum, ('rec', 'src'))  197 us
    all_gather x2, waiting for transfers between devices, on_device(): forward_spread = lax.all_gather(right_unit, 'rec', axis=0, tiled=True)  172 us
    all_gather x1, waiting for transfers between devices, on_device(): piece_traces = lax.all_gather(traces, 'rec', axis=1, tiled=True)  112 us
    reduce_scatter x2, waiting for transfers between devices, on_device(): lax.psum_scatter(kernel_apply(kernel, forward_spread), 'src', scatter_dim...  65.9 us
    all_gather x2, waiting for transfers between devices, adjoint(): spread = lax.all_gather(vector, 'src', axis=0, tiled=True)  52.6 us
    unnamed x1, blocking collectives  40.1 us
    dot_general x2, matrix products, kernel_adjoint(): jnp.einsum('fmc,mfn->cfn', kernel[1], vector[:, 0], precision=highest)  26.3 us
  transfers between devices with their start and end apart: 9, of which 9 were waited for; matrix products, arithmetic and copies ran while one was open for 0% of the time, Pallas kernels for 0%

commit v1 on v0

v1 whole, which is shorter than its diff:
```python
import functools
import jax
import jax.numpy as jnp
from jax import lax
from jax.experimental import pallas as pl
from jax.experimental.pallas import tpu as pltpu
from jax.sharding import Mesh, PartitionSpec as P

FREQS = 2
SOURCES = 256
ITERS = 2
HEAD = 8
REC = ("z", "y")
SRC = ("x", "c")
VMEM_BYTES = 50 * 2**20


def split(values):
    high = values.astype(jnp.bfloat16)
    return high, (values - high.astype(jnp.float32)).astype(jnp.bfloat16)


def dot_three(left, right, dims):
    def dot(a, b):
        return lax.dot_general(a, b, (dims, ((), ())), preferred_element_type=jnp.float32)

    return dot(left[0], right[0]) + (dot(left[0], right[1]) + dot(left[1], right[0]))


def dot_exact(chosen, values):
    total = None
    for _ in range(3):
        part = values.astype(jnp.bfloat16)
        values = values - part.astype(jnp.float32)
        term = lax.dot_general(
            chosen, part, (((0,), (0,)), ((), ())), preferred_element_type=jnp.float32
        )
        total = term if total is None else total + term
    return total


def xor_index(axis, k):
    index = lax.axis_index(axis)
    if k == 0:
        return index
    if k == 1:
        return index + 1 - 2 * lax.rem(index, 2)
    if k == 3:
        return 3 - index
    return lax.rem(index + 2, 4)


def product_kernel(adjoint, places, outs, k_ref, *refs):
    piece_refs = refs[: len(places)]
    out_refs = refs[len(places) : len(places) + len(outs)]
    head, high, low, total = refs[len(places) + len(outs) :]
    step = pl.program_id(0)

    @pl.when(step == 0)
    def _():
        sums = None
        for place, piece in zip(places, piece_refs):
            rows = piece.shape[0] - HEAD
            at = 0 if place is None else pl.multiple_of(place() * rows, rows)
            top, bottom = split(piece[HEAD:, :])
            high[pl.ds(at, rows), :] = top
            low[pl.ds(at, rows), :] = bottom
            sums = piece[:HEAD, :] if sums is None else sums + piece[:HEAD, :]
        head[...] = sums

    dims = ((0,), (0,)) if adjoint else ((1,), (0,))
    vector = (high[...], low[...])
    with_real = dot_three(split(k_ref[0, 0]), vector, dims)
    with_imag = dot_three(split(k_ref[1, 0]), vector, dims)
    rows, half = with_real.shape[0], with_real.shape[1] // 2
    at = pl.multiple_of(step * rows, rows)
    if adjoint:
        total[pl.ds(at, rows), :half] = with_real[:, :half] + with_imag[:, half:]
        total[pl.ds(at, rows), half:] = with_real[:, half:] - with_imag[:, :half]
    else:
        total[pl.ds(at, rows), :half] = with_real[:, :half] - with_imag[:, half:]
        total[pl.ds(at, rows), half:] = with_real[:, half:] + with_imag[:, :half]

    @pl.when(step == pl.num_programs(0) - 1)
    def _():
        for out, out_ref in zip(outs, out_refs):
            for slot, place in enumerate(out):
                target = out_ref.at[slot] if len(out) > 1 else out_ref
                rows = target.shape[0] - HEAD
                at = 0 if place is None else pl.multiple_of(place() * rows, rows)
                target[:HEAD, :] = head[...]
                target[HEAD:, :] = total[pl.ds(at, rows), :]


def product(kernel, slab, adjoint, pieces, places, outs, out_rows):
    rows, columns = kernel.shape[2:]
    width = pieces[0].shape[1]
    if adjoint:
        tile = columns // 2 if columns % 256 == 0 and columns > 640 else columns
        steps, shape, given, made = columns // tile, (2, 1, rows, tile), rows, columns
        k_spec = pl.BlockSpec(shape, lambda i: (0, slab, 0, i))
    else:
        tile = rows // 4
        steps, shape, given, made = rows // tile, (2, 1, tile, columns), columns, rows
        k_spec = pl.BlockSpec(shape, lambda i: (0, slab, i, 0))
    shapes = [
        ((len(out),) if len(out) > 1 else ()) + (out_rows + HEAD, width) for out in outs
    ]
    return pl.pallas_call(
        functools.partial(product_kernel, adjoint, places, outs),
        grid=(steps,),
        in_specs=[k_spec] + [pl.BlockSpec(p.shape, lambda i: (0, 0)) for p in pieces],
        out_specs=[pl.BlockSpec(s, lambda i, n=len(s): (0,) * n) for s in shapes],
        out_shape=[jax.ShapeDtypeStruct(s, jnp.float32) for s in shapes],
        scratch_shapes=[
            pltpu.VMEM((HEAD, width), jnp.float32),
            pltpu.VMEM((given, width), jnp.bfloat16),
            pltpu.VMEM((given, width), jnp.bfloat16),
            pltpu.VMEM((made, width), jnp.float32),
        ],
        compiler_params=pltpu.CompilerParams(vmem_limit_bytes=VMEM_BYTES),
        cost_estimate=pl.CostEstimate(
            flops=2 * 3 * 2 * rows * columns * width,
            bytes_accessed=8 * rows * columns + 4 * width * (rows + columns),
            transcendentals=0,
        ),
    )(kernel, *pieces)


def finish_kernel(count, parts, *refs):
    part_refs, refs = refs[:parts], refs[parts:]
    piece_ref, norm_ref = refs[-2:]
    total = part_refs[0][...]
    for part in part_refs[1:]:
        total = total + part[...]
    norm = jnp.sqrt(total[:1, :1] / count)
    data = total[HEAD:, :] / norm
    if len(refs) > 2:
        other, last_norm = refs[:2]
        data = data - norm * (other[HEAD:, :] / last_norm[:1, :1])
    piece_ref[HEAD:, :] = data
    piece_ref[:HEAD, :] = jnp.broadcast_to(jnp.sum(data * data), (HEAD, data.shape[1]))
    norm_ref[...] = jnp.broadcast_to(norm, norm_ref.shape)


def finish(count, parts, *other):
    shape = parts[0].shape
    return pl.pallas_call(
        functools.partial(finish_kernel, count, len(parts)),
        out_shape=[
            jax.ShapeDtypeStruct(shape, jnp.float32),
            jax.ShapeDtypeStruct((8, 128), jnp.float32),
        ],
        compiler_params=pltpu.CompilerParams(vmem_limit_bytes=VMEM_BYTES),
        cost_estimate=pl.CostEstimate(
            flops=shape[0] * shape[1] * 8,
            bytes_accessed=4 * shape[0] * shape[1] * (len(parts) + 2),
            transcendentals=0,
        ),
    )(*parts, *other)


def pack_kernel(place_ref, mark_ref, traces_ref, first_ref, second_ref):
    slots = first_ref.shape[0]
    spots = lax.broadcasted_iota(jnp.int32, (place_ref.shape[0], slots), 1)
    chosen = (place_ref[...] == spots).astype(jnp.bfloat16)
    width = second_ref.shape[1]
    half = width // 2
    packed = dot_exact(chosen, traces_ref[...])
    marks = jnp.broadcast_to(mark_ref[...], (mark_ref.shape[0], 128))
    first_ref[:, :half] = packed[:, :half]
    first_ref[:, half:width] = packed[:, width : width + half]
    first_ref[:, width:] = dot_exact(chosen, marks)
    second_ref[:, :half] = packed[:, half:width]
    second_ref[:, half:] = packed[:, width + half :]


def unpack_kernel(data_ref, mark_ref, piece_ref):
    rows = piece_ref.shape[0] - HEAD
    width = piece_ref.shape[1]
    slots = data_ref.shape[0]
    spots = lax.broadcasted_iota(jnp.int32, (slots, rows), 1) + 1
    chosen = (mark_ref[:, :1].astype(jnp.int32) == spots).astype(jnp.bfloat16)
    data = dot_exact(chosen, data_ref[:, :width])
    piece_ref[HEAD:, :] = data
    piece_ref[:HEAD, :] = jnp.broadcast_to(jnp.sum(data * data), (HEAD, width))


def dispatch(traces, acq_lists, counts, row_count):
    areas = lax.axis_size("z") * lax.axis_size("y")
    slot_count = traces.shape[1]
    width = traces.shape[2] * traces.shape[4]
    peer = -(-slot_count // areas)
    ids = acq_lists[0]
    slot_iota = jnp.arange(slot_count, dtype=jnp.int32)
    area = jnp.where(slot_iota < counts[0, 0], ids // row_count, -1)
    before = (area[:, None] == area[None, :]) & (slot_iota[None, :] < slot_iota[:, None])
    rank = jnp.sum(before.astype(jnp.int32), axis=1)
    place = jnp.where(area >= 0, area * peer + rank, -1)
    mark = (ids % row_count + 1).astype(jnp.float32)
    params = pltpu.CompilerParams(vmem_limit_bytes=VMEM_BYTES)
    slots = areas * peer
    first, second = pl.pallas_call(
        pack_kernel,
        out_shape=[
            jax.ShapeDtypeStruct((slots, width + 128), jnp.float32),
            jax.ShapeDtypeStruct((slots, width), jnp.float32),
        ],
        compiler_params=params,
    )(place[:, None], mark[:, None], traces.reshape(slot_count, -1))

    def exchange(packed):
        packed = packed.reshape(areas, peer, -1)
        packed = lax.all_to_all(packed, REC, 0, 0, tiled=True)
        return packed.reshape(slots, -1)

    unpack = pl.pallas_call(
        unpack_kernel,
        out_shape=jax.ShapeDtypeStruct((row_count + HEAD, width), jnp.float32),
        compiler_params=params,
    )
    first = exchange(first)
    marks = first[:, width:]
    second = exchange(second)
    return [unpack(first, marks), unpack(second, marks)]


def swap(values, axis, k=1):
    size = lax.axis_size(axis)
    return lax.ppermute(values, axis, [(i, i ^ k) for i in range(size)])


def rec_place(kz, ky):
    return lambda: xor_index("z", kz) * 2 + xor_index("y", ky)


def src_place(kx, kc):
    return lambda: xor_index("x", kx) * 2 + xor_index("c", kc)


class Neighbours:
    def gather_src(self, piece, slab):
        x = swap(piece, "x")
        c = swap(piece, "c")
        xc = swap(x, "c")
        return [piece, x, c, xc], [src_place(*k) for k in ((0, 0), (1, 0), (0, 1), (1, 1))]

    def gather_rec(self, piece, slab):
        one, three, side = swap(piece, "z", 1), swap(piece, "z", 3), swap(piece, "y")
        two = swap(three, "z", 1)
        side_three = swap(side, "z", 3)
        side_one = swap(one, "y")
        side_two = swap(two, "y") if slab == 0 else swap(side_three, "z", 1)
        order = ((0, 0), (1, 0), (3, 0), (2, 0), (0, 1), (1, 1), (3, 1), (2, 1))
        return [piece, one, three, two, side, side_one, side_three, side_two], [
            rec_place(*k) for k in order
        ]

    rec_outs = [[rec_place(*k)] for k in ((2, 1), (3, 1), (1, 1), (2, 0))] + [
        [rec_place(*k)] for k in ((0, 0), (1, 0), (3, 0), (0, 1))
    ]
    src_outs = [[src_place(0, 1), src_place(1, 1)], [src_place(1, 0)], [src_place(0, 0)]]

    def scatter_rec(self, blocks, slab):
        side_two, side_three, side_one, two, own, one, three, side = blocks
        if slab == 0:
            two = two + swap(side_two, "y")
        else:
            side_three = side_three + swap(side_two, "z", 1)
        one = one + swap(side_one, "y")
        side = side + swap(side_three, "z", 3)
        three = three + swap(two, "z", 1)
        return [own, swap(one, "z", 1), swap(three, "z", 3), swap(side, "y")]

    def scatter_src(self, blocks, slab):
        sent, across, own = blocks
        back = swap(sent, "c")
        return [own, back[0], swap(across + back[1], "x")]


class Whole:
    rec_outs = [[None]]
    src_outs = [[None]]

    def gather(self, piece, axes):
        pieces = lax.all_gather(piece, axes, axis=0, tiled=False)
        data = pieces[:, HEAD:].reshape(-1, piece.shape[1])
        return [jnp.concatenate([jnp.sum(pieces[:, :HEAD], axis=0), data], axis=0)], [None]

    def scatter(self, blocks, axes):
        count = lax.axis_size(axes[0]) * lax.axis_size(axes[1])
        width = blocks[0].shape[1]
        head = jnp.broadcast_to(blocks[0][:HEAD], (count, HEAD, width))
        data = blocks[0][HEAD:].reshape(count, -1, width)
        both = jnp.concatenate([head, data], axis=1)
        return [lax.psum_scatter(both, axes, scatter_dimension=0, tiled=False)]

    def gather_src(self, piece, slab):
        return self.gather(piece, SRC)

    def gather_rec(self, piece, slab):
        return self.gather(piece, REC)

    def scatter_rec(self, blocks, slab):
        return self.scatter(blocks, REC)

    def scatter_src(self, blocks, slab):
        return self.scatter(blocks, SRC)


def global_sum(values):
    for axis in ("c", "x", "y", "z"):
        k = 1
        while k < lax.axis_size(axis):
            values = values + swap(values, axis, 2 * k - 1)
            k *= 2
    return values


def on_device(kernel, traces, acq_lists, counts):
    sizes = tuple(lax.axis_size(axis) for axis in ("z", "y", "x", "c"))
    row_count = kernel.shape[2] // (sizes[2] * sizes[3])
    column_count = kernel.shape[3] // (sizes[0] * sizes[1])
    aligned = row_count % 16 == 0 and column_count % 16 == 0
    moves = Neighbours() if sizes == (4, 2, 2, 2) and aligned else Whole()
    count = 2.0 * kernel.shape[2] * sizes[0] * sizes[1] * SOURCES

    def adjoint(piece, slab):
        pieces, places = moves.gather_src(piece, slab)
        rows = column_count if len(moves.rec_outs) > 1 else kernel.shape[3]
        blocks = product(kernel, slab, True, pieces, places, moves.rec_outs, rows)
        return moves.scatter_rec(blocks, slab)

    def forward(piece, slab):
        pieces, places = moves.gather_rec(piece, slab)
        rows = row_count if len(moves.src_outs) > 1 else kernel.shape[2]
        blocks = product(kernel, slab, False, pieces, places, moves.src_outs, rows)
        return moves.scatter_src(blocks, slab)

    observed = dispatch(traces, acq_lists, counts, row_count)
    solutions, lefts = [], []
    for slab in range(FREQS):
        left = observed[slab]
        right, beta = finish(count, adjoint(left, slab))
        phibar = beta[0, 0]
        search = None
        for iteration in range(ITERS):
            left, alpha = finish(count, forward(right, slab), left, beta)
            unit = right[HEAD:] / alpha[0, 0]
            if iteration == 0:
                rhobar = alpha[0, 0]
                search = unit
            else:
                rhobar = -cosine * alpha[0, 0]
                search = unit - (sine * alpha[0, 0] / rho) * search
            if iteration + 1 < ITERS:
                right, beta = finish(count, adjoint(left, slab), right, alpha)
                beta_norm = beta[0, 0]
            else:
                beta_norm = jnp.sqrt(global_sum(left[:HEAD, :128])[0, 0] / count)
            rho = jnp.sqrt(rhobar * rhobar + beta_norm * beta_norm)
            cosine = rhobar / rho
            sine = beta_norm / rho
            phi = cosine * phibar
            phibar = sine * phibar
            step = (phi / rho) * search
            solution = step if iteration == 0 else solution + step
        solutions.append(solution)
        lefts.append(left[HEAD:])

    def joined(parts):
        return jnp.stack([p.reshape(p.shape[0], 2, SOURCES) for p in parts], axis=2)

    return joined(solutions), joined(lefts)


def solution(mesh):
    rec, src = mesh.shape["rec"], mesh.shape["src"]
    depth = src // 2
    fine = Mesh(
        mesh.devices.reshape(rec // depth, depth, depth, 2), REC + SRC
    )
    placed = (
        P(None, None, REC, SRC),
        P(SRC, REC, None, None, None),
        P(SRC, REC),
        P(SRC, REC),
    )
    return jax.shard_map(
        on_device,
        mesh=fine,
        in_specs=placed,
        out_specs=(P(SRC + REC, None, None, None), P(REC + SRC, None, None, None)),
        check_vma=False,
    )
```

time: 1080 us -> 480 us (0.44)
  waiting for transfers between devices: 608 us -> 216 us
  blocking collectives: 238 us -> 28.7 us
  matrix products: 173 us -> 0 us
  starting transfers between devices: 0.59 us -> 122 us
  Pallas kernels: 0 us -> 74.4 us
  other arithmetic: 22.7 us -> 7.73 us
  local copies, waits for them, and re-layouts: 21.3 us -> 9.92 us
    all_gather x5 -> x0, waiting for transfers between devices: 336 us -> none  [the longest x2 172 us: on_device(): forward_spread = lax.all_gather(right_unit, 'rec', axis=0, tiled=True)]
    reduce_scatter x4 -> x0, waiting for transfers between devices: 271 us -> none  [the longest x2 206 us: adjoint(): lax.psum_scatter(kernel_adjoint(kernel, spread), 'rec', scatter_dimension...]
    ppermute x0 -> x86, waiting for transfers between devices: none -> 202 us  [swap(): return lax.ppermute(values, axis, [(i, i ^ k) for i in range(size)])]
    psum x5 -> x0, blocking collectives: 197 us -> none  [rms_norm(): global_sum = lax.psum(local_sum, ('rec', 'src'))]
    dot_general x17 -> x0, matrix products: 173 us -> none  [the longest x2 26.3 us: kernel_adjoint(): jnp.einsum('fmc,mfn->cfn', kernel[1], vector[:, 0], precision=highest)]
    ppermute x0 -> x86, starting transfers between devices: none -> 119 us  [swap(): return lax.ppermute(values, axis, [(i, i ^ k) for i in range(size)])]
    pallas_call x0 -> x19, Pallas kernels: none -> 74.4 us  [the longest x8 67.7 us: product(): pl.pallas_call(functools.partial(product_kernel, adjoint, places, outs),...]
    unnamed x1 -> x0, blocking collectives: 40.1 us -> none
  transfers between devices with their start and end apart: 9 -> 87, of which waited for: 9 -> 32; matrix products, arithmetic and copies ran while one was open for 0% -> 2% of each run, Pallas kernels for 0% -> 15%
where the time goes in v1:
time: 480 us; the launch traced here: 476 us
  waiting for transfers between devices  216 us (45%)
  starting transfers between devices  122 us (25%)
  Pallas kernels  74.4 us (16%)
  blocking collectives  28.7 us (6%)
  between operations  17.2 us (4%)
  local copies, waits for them, and re-layouts  9.92 us (2%)
  other arithmetic  7.73 us (2%)
    ppermute x86, waiting for transfers between devices, swap(): return lax.ppermute(values, axis, [(i, i ^ k) for i in range(size)])  202 us
    ppermute x86, starting transfers between devices, swap(): return lax.ppermute(values, axis, [(i, i ^ k) for i in range(size)])  119 us
    pallas_call x8, Pallas kernels, product(): pl.pallas_call(functools.partial(product_kernel, adjoint, places, outs),...  67.7 us
    all_to_all x1, blocking collectives, exchange(): packed = lax.all_to_all(packed, REC, 0, 0, tiled=True)  28.7 us
    all_to_all x1, waiting for transfers between devices, exchange(): packed = lax.all_to_all(packed, REC, 0, 0, tiled=True)  14.2 us
  transfers between devices with their start and end apart: 87, of which 32 were waited for; matrix products, arithmetic and copies ran while one was open for 2% of the time, Pallas kernels for 15%

profile of v1, /device:TPU:0, one launch (start us, length us, event | category | flops | bytes accessed | tf_op | source)
XLA Modules:
  0.0 476.1 jit_solution(5554062773778909057)
XLA Ops:
  3.2 2.3 reshape.151.traces_ref
  5.9 2.2 shard_map.59
  8.1 28.7 %all_to_all.10 = f32[8,40,640]{2,1,0:T(8,128)S(1)} all-to-all(f32[8,40,640]{2,1,0:T(8,128)S(1)} %bitcast.50), channel_id=1, replica_groups=mesh['z'=4,'y'=2,'x'=2,'c'=2] {'z','y'}, dimensions={0} | all-to-all | bytes 1638400 | tf_op jit(solution)/shard_map/all_to_all | solution.py:214
  36.7 3.7 all-to-all-start.1
  41.2 1.6 collective-permute-start
  42.8 14.2 %all-to-all-done.1 = f32[8,40,512]{2,1,0:T(8,128)S(1)} async-done(((f32[8,40,512]{2,1,0:T(8,128)}), f32[8,40,512]{2,1,0:T(8,128)S(1)}, u32[]{:S(2)}, u32[]{:S(2)}) %all-to-all-start.1) | async-done | bytes 655392 | tf_op jit(solution)/shard_map/all_to_all | solution.py:214
  59.8 5.8 %collective-permute-done.43.refs_1_ = f32[168,512]{1,0:T(8,128)S(1)} collective-permute-done((f32[168,512]{1,0:T(8,128)S(1)}, f32[168,512]{1,0:T(8,128)S(1)}, u32[]{:S(2)}, u32[]{:S(2)}) %collective-permute-start.43) | collective-permute-done | bytes 344096 | tf_op jit(solution)/shard_map/ppermute | solution.py:230
  65.7 9.0 %shard_map.61 = (f32[168,512]{1,0:T(8,128)S(1)}, f32[168,512]{1,0:T(8,128)S(1)}, f32[168,512]{1,0:T(8,128)S(1)}, f32[168,512]{1,0:T(8,128)S(1)}, f32[168,512]{1,...) custom-call(f32[2,2,640,1280]{3,2,1,0:T(8,128)} %k_ref.15, ...), custom_call_target="tpu_custom_call" | custom-call | flops 5033164800 | bytes 10485760 | tf_op jit(solution)/shard_map/pallas_call | solution.py:109
  74.6 2.2 collective-permute-start.8
  76.8 2.7 collective-permute-start.5
  79.5 8.9 %shard_map.70 = (f32[168,512]{1,0:T(8,128)S(1)}, f32[168,512]{1,0:T(8,128)S(1)}, f32[168,512]{1,0:T(8,128)S(1)}, f32[168,512]{1,0:T(8,128)S(1)}, f32[168,512]{1,...) custom-call(f32[2,2,640,1280]{3,2,1,0:T(8,128)} %k_ref.15, ...), custom_call_target="tpu_custom_call" | custom-call | flops 5033164800 | bytes 10485760 | tf_op jit(solution)/shard_map/pallas_call | solution.py:109
  88.7 2.0 collective-permute-start.6
  90.8 2.0 collective-permute-start.46
  92.9 6.6 %collective-permute-done.50 = f32[168,512]{1,0:T(8,128)S(1)} collective-permute-done((f32[168,512]{1,0:T(8,128)S(1)}, f32[168,512]{1,0:T(8,128)S(1)}, u32[]{:S(2)}, u32[]{:S(2)}) %collective-permute-start.50) | collective-permute-done | bytes 344096 | tf_op jit(solution)/shard_map/ppermute | solution.py:230
  101.0 5.8 %collective-permute-done.6 = f32[168,512]{1,0:T(8,128)S(1)} collective-permute-done((f32[168,512]{1,0:T(8,128)S(1)}, f32[168,512]{1,0:T(8,128)S(1)}, u32[]{:S(2)}, u32[]{:S(2)}) %collective-permute-start.6) | collective-permute-done | bytes 344096 | tf_op jit(solution)/shard_map/ppermute | solution.py:230
  106.9 14.7 %collective-permute-done.48 = f32[168,512]{1,0:T(8,128)S(1)} collective-permute-done((f32[168,512]{1,0:T(8,128)S(1)}, f32[168,512]{1,0:T(8,128)S(1)}, u32[]{:S(2)}, u32[]{:S(2)}) %collective-permute-start.48) | collective-permute-done | bytes 344096 | tf_op jit(solution)/shard_map/ppermute | solution.py:230
  122.6 3.0 collective-permute-start.49
  125.8 17.9 %collective-permute-done.4.refs_1_ = f32[168,512]{1,0:T(8,128)S(1)} collective-permute-done((f32[168,512]{1,0:T(8,128)S(1)}, f32[168,512]{1,0:T(8,128)S(1)}, u32[]{:S(2)}, u32[]{:S(2)}) %collective-permute-start.4) | collective-permute-done | bytes 344096 | tf_op jit(solution)/shard_map/ppermute | solution.py:230
  145.0 2.3 collective-permute-start.10
  147.3 11.2 %collective-permute-done.47.refs_1_ = f32[168,512]{1,0:T(8,128)S(1)} collective-permute-done((f32[168,512]{1,0:T(8,128)S(1)}, f32[168,512]{1,0:T(8,128)S(1)}, u32[]{:S(2)}, u32[]{:S(2)}) %collective-permute-start.47) | collective-permute-done | bytes 344096 | tf_op jit(solution)/shard_map/ppermute | solution.py:230
  159.8 16.5 %collective-permute-start.12 = (f32[168,512]{1,0:T(8,128)S(1)}, f32[168,512]{1,0:T(8,128)S(1)}, u32[]{:S(2)}, u32[]{:S(2)}) collective-permute-start(f32[168,512]{1,0:T(8,128)S(1)} %collective-permute-done.11.refs_2_), channel_id=1, source_target_pairs={{0,8},{8,0},{16,24},{24,16},{1,9},{9,1},{17,25},{25,17},{2,10},{10... | collective-permute-start | bytes 1032200 | tf_op jit(solution)/shard_map/ppermute | solution.py:230
  177.3 2.9 collective-permute-start.15
  180.3 7.4 %collective-permute-done.12.refs_3_ = f32[168,512]{1,0:T(8,128)S(1)} collective-permute-done((f32[168,512]{1,0:T(8,128)S(1)}, f32[168,512]{1,0:T(8,128)S(1)}, u32[]{:S(2)}, u32[]{:S(2)}) %collective-permute-start.12) | collective-permute-done | bytes 344096 | tf_op jit(solution)/shard_map/ppermute | solution.py:230
  187.6 16.0 %collective-permute-done.53.refs_1_ = f32[168,512]{1,0:T(8,128)S(1)} collective-permute-done((f32[168,512]{1,0:T(8,128)S(1)}, f32[168,512]{1,0:T(8,128)S(1)}, u32[]{:S(2)}, u32[]{:S(2)}) %collective-permute-start.53) | collective-permute-done | bytes 344096 | tf_op jit(solution)/shard_map/ppermute | solution.py:230
  203.6 2.1 collective-permute-start.59
  205.7 2.6 collective-permute-done.15.refs_6_
  208.3 8.1 %shard_map.63 = (f32[2,168,512]{2,1,0:T(8,128)S(1)}, f32[168,512]{1,0:T(8,128)S(1)}, f32[168,512]{1,0:T(8,128)S(1)}) custom-call(f32[2,2,640,1280]{3,2,1,0:T(8,128)} %k_ref.15, f32[168,512]{1,0:T(8,128)S(1)} %get-tuple-element.73.refs_0_.refs_4_, f32[168,512]{1,0:T(8,128)S(1)} %collective-permute-done.10.refs_1_, ...), custom_call_target="tpu_custom_call" | custom-call | flops 5033164800 | bytes 10485760 | tf_op jit(solution)/shard_map/pallas_call | solution.py:109
  216.5 7.9 %shard_map.72 = (f32[2,168,512]{2,1,0:T(8,128)S(1)}, f32[168,512]{1,0:T(8,128)S(1)}, f32[168,512]{1,0:T(8,128)S(1)}) custom-call(f32[2,2,640,1280]{3,2,1,0:T(8,128)} %k_ref.15, f32[168,512]{1,0:T(8,128)S(1)} %get-tuple-element.104.refs_0_.refs_4_, f32[168,512]{1,0:T(8,128)S(1)} %collective-permute-done.53.refs_1_, ...), custom_call_target="tpu_custom_call" | custom-call | flops 5033164800 | bytes 10485760 | tf_op jit(solution)/shard_map/pallas_call | solution.py:109
  226.8 1.6 collective-permute-start.61
  228.3 7.6 %collective-permute-done.18.refs_2_ = f32[168,512]{1,0:T(8,128)S(1)} collective-permute-done((f32[168,512]{1,0:T(8,128)S(1)}, f32[168,512]{1,0:T(8,128)S(1)}, u32[]{:S(2)}, u32[]{:S(2)}) %collective-permute-start.18) | collective-permute-done | bytes 344096 | tf_op jit(solution)/shard_map/ppermute | solution.py:230
  237.9 5.4 %collective-permute-done.61.refs_2_ = f32[168,512]{1,0:T(8,128)S(1)} collective-permute-done((f32[168,512]{1,0:T(8,128)S(1)}, f32[168,512]{1,0:T(8,128)S(1)}, u32[]{:S(2)}, u32[]{:S(2)}) %collective-permute-start.61) | collective-permute-done | bytes 344096 | tf_op jit(solution)/shard_map/ppermute | solution.py:230
  245.3 5.4 %collective-permute-done.19.refs_1_ = f32[168,512]{1,0:T(8,128)S(1)} collective-permute-done((f32[168,512]{1,0:T(8,128)S(1)}, f32[168,512]{1,0:T(8,128)S(1)}, u32[]{:S(2)}, u32[]{:S(2)}) %collective-permute-start.19) | collective-permute-done | bytes 344096 | tf_op jit(solution)/shard_map/ppermute | solution.py:230
  251.2 5.9 %collective-permute-done.62.refs_1_ = f32[168,512]{1,0:T(8,128)S(1)} collective-permute-done((f32[168,512]{1,0:T(8,128)S(1)}, f32[168,512]{1,0:T(8,128)S(1)}, u32[]{:S(2)}, u32[]{:S(2)}) %collective-permute-start.62) | collective-permute-done | bytes 344096 | tf_op jit(solution)/shard_map/ppermute | solution.py:230
  257.2 9.0 %shard_map.65 = (f32[168,512]{1,0:T(8,128)S(1)}, f32[168,512]{1,0:T(8,128)S(1)}, f32[168,512]{1,0:T(8,128)S(1)}, f32[168,512]{1,0:T(8,128)S(1)}, f32[168,512]{1,...) custom-call(f32[2,2,640,1280]{3,2,1,0:T(8,128)} %k_ref.15, ...), custom_call_target="tpu_custom_call" | custom-call | flops 5033164800 | bytes 10485760 | tf_op jit(solution)/shard_map/pallas_call | solution.py:109
  266.2 3.0 collective-permute-start.27
  269.1 9.2 %shard_map.74 = (f32[168,512]{1,0:T(8,128)S(1)}, f32[168,512]{1,0:T(8,128)S(1)}, f32[168,512]{1,0:T(8,128)S(1)}, f32[168,512]{1,0:T(8,128)S(1)}, f32[168,512]{1,...) custom-call(f32[2,2,640,1280]{3,2,1,0:T(8,128)} %k_ref.15, ...), custom_call_target="tpu_custom_call" | custom-call | flops 5033164800 | bytes 10485760 | tf_op jit(solution)/shard_map/pallas_call | solution.py:109
  278.4 2.1 collective-permute-start.22
  280.5 2.0 collective-permute-start.25
  282.7 6.6 %collective-permute-done.69 = f32[168,512]{1,0:T(8,128)S(1)} collective-permute-done((f32[168,512]{1,0:T(8,128)S(1)}, f32[168,512]{1,0:T(8,128)S(1)}, u32[]{:S(2)}, u32[]{:S(2)}) %collective-permute-start.69) | collective-permute-done | bytes 344096 | tf_op jit(solution)/shard_map/ppermute | solution.py:230
  289.3 2.0 collective-permute-start.28
  292.4 4.2 collective-permute-done.25
  296.7 14.7 %collective-permute-done.67 = f32[168,512]{1,0:T(8,128)S(1)} collective-permute-done((f32[168,512]{1,0:T(8,128)S(1)}, f32[168,512]{1,0:T(8,128)S(1)}, u32[]{:S(2)}, u32[]{:S(2)}) %collective-permute-start.67) | collective-permute-done | bytes 344096 | tf_op jit(solution)/shard_map/ppermute | solution.py:230
  311.5 3.9 collective-permute-start.68
  315.6 2.1 collective-permute-start.71
  317.7 15.9 %collective-permute-done.23.refs_1_ = f32[168,512]{1,0:T(8,128)S(1)} collective-permute-done((f32[168,512]{1,0:T(8,128)S(1)}, f32[168,512]{1,0:T(8,128)S(1)}, u32[]{:S(2)}, u32[]{:S(2)}) %collective-permute-start.23) | collective-permute-done | bytes 344096 | tf_op jit(solution)/shard_map/ppermute | solution.py:230
  334.0 3.1 collective-permute-start.29
  337.1 2.2 collective-permute-start.32
  339.3 9.0 %collective-permute-done.66.refs_1_ = f32[168,512]{1,0:T(8,128)S(1)} collective-permute-done((f32[168,512]{1,0:T(8,128)S(1)}, f32[168,512]{1,0:T(8,128)S(1)}, u32[]{:S(2)}, u32[]{:S(2)}) %collective-permute-start.66) | collective-permute-done | bytes 344096 | tf_op jit(solution)/shard_map/ppermute | solution.py:230
  348.7 2.1 collective-permute-start.75
  350.8 15.3 %collective-permute-start.31 = (f32[168,512]{1,0:T(8,128)S(1)}, f32[168,512]{1,0:T(8,128)S(1)}, u32[]{:S(2)}, u32[]{:S(2)}) collective-permute-start(f32[168,512]{1,0:T(8,128)S(1)} %collective-permute-done.30.refs_2_), channel_id=1, source_target_pairs={{0,8},{8,0},{16,24},{24,16},{1,9},{9,1},{17,25},{25,17},{2,10},{10... | collective-permute-start | bytes 1032200 | tf_op jit(solution)/shard_map/ppermute | solution.py:230
  366.1 2.2 collective-permute-start.33
  369.2 2.9 collective-permute-start.34
  372.1 5.5 %collective-permute-done.31.refs_3_ = f32[168,512]{1,0:T(8,128)S(1)} collective-permute-done((f32[168,512]{1,0:T(8,128)S(1)}, f32[168,512]{1,0:T(8,128)S(1)}, u32[]{:S(2)}, u32[]{:S(2)}) %collective-permute-start.31) | collective-permute-done | bytes 344096 | tf_op jit(solution)/shard_map/ppermute | solution.py:230
  377.6 3.1 collective-permute-start.35
  380.7 12.7 %collective-permute-done.72.refs_1_ = f32[168,512]{1,0:T(8,128)S(1)} collective-permute-done((f32[168,512]{1,0:T(8,128)S(1)}, f32[168,512]{1,0:T(8,128)S(1)}, u32[]{:S(2)}, u32[]{:S(2)}) %collective-permute-start.72) | collective-permute-done | bytes 344096 | tf_op jit(solution)/shard_map/ppermute | solution.py:230
  393.4 2.2 collective-permute-start.76
  395.6 2.0 collective-permute-start.78
  398.1 7.9 %shard_map.67 = (f32[2,168,512]{2,1,0:T(8,128)S(1)}, f32[168,512]{1,0:T(8,128)S(1)}, f32[168,512]{1,0:T(8,128)S(1)}) custom-call(f32[2,2,640,1280]{3,2,1,0:T(8,128)} %k_ref.15, f32[168,512]{1,0:T(8,128)S(1)} %get-tuple-element.89.refs_0_, f32[168,512]{1,0:T(8,128)S(1)} %collective-permute-done.29.refs_1_, f32[168,512]{1,0:T(8,128)S(1)} %collective-permute-done.30.refs_2_, ...), custom_call_target="tpu_custom_call" | custom-call | flops 5033164800 | bytes 10485760 | tf_op jit(solution)/shard_map/pallas_call | solution.py:109
  406.5 7.9 %shard_map.76 = (f32[2,168,512]{2,1,0:T(8,128)S(1)}, f32[168,512]{1,0:T(8,128)S(1)}, f32[168,512]{1,0:T(8,128)S(1)}) custom-call(f32[2,2,640,1280]{3,2,1,0:T(8,128)} %k_ref.15, f32[168,512]{1,0:T(8,128)S(1)} %get-tuple-element.120.refs_0_, f32[168,512]{1,0:T(8,128)S(1)} %collective-permute-done.72.refs_1_, f32[168,512]{1,0:T(8,128)S(1)} %collective-permute-done.73.refs_2_, ...), custom_call_target="tpu_custom_call" | custom-call | flops 5033164800 | bytes 10485760 | tf_op jit(solution)/shard_map/pallas_call | solution.py:109
  418.2 7.3 %collective-permute-done.37.refs_2_ = f32[168,512]{1,0:T(8,128)S(1)} collective-permute-done((f32[168,512]{1,0:T(8,128)S(1)}, f32[168,512]{1,0:T(8,128)S(1)}, u32[]{:S(2)}, u32[]{:S(2)}) %collective-permute-start.37) | collective-permute-done | bytes 344096 | tf_op jit(solution)/shard_map/ppermute | solution.py:230
  426.0 6.4 %collective-permute-done.80.refs_2_ = f32[168,512]{1,0:T(8,128)S(1)} collective-permute-done((f32[168,512]{1,0:T(8,128)S(1)}, f32[168,512]{1,0:T(8,128)S(1)}, u32[]{:S(2)}, u32[]{:S(2)}) %collective-permute-start.80) | collective-permute-done | bytes 344096 | tf_op jit(solution)/shard_map/ppermute | solution.py:230
  436.6 1.7 collective-permute-start.40
  443.8 2.6 collective-permute-start.42
  473.4 2.2 pad_maximum_fusion
  (195 shorter events, 49.9 us)
Async XLA Ops:
  36.7 20.3 %all-to-all-start.1 = ((f32[8,40,512]{2,1,0:T(8,128)}), f32[8,40,512]{2,1,0:T(8,128)S(1)}, u32[]{:S(2)}, u32[]{:S(2)}) async-start(f32[8,40,512]{2,1,0:T(8,128)} %bitcast.15), calls=%async_computation.1 | async-start | bytes 1310720 | tf_op jit(solution)/shard_map/all_to_all | solution.py:214
  41.2 18.1 %collective-permute-start = (f32[168,512]{1,0:T(8,128)S(1)}, f32[168,512]{1,0:T(8,128)S(1)}, u32[]{:S(2)}, u32[]{:S(2)}) collective-permute-start(f32[168,512]{1,0:T(8,128)S(1)} %shard_map.60.refs_0_.refs_3_), channel_id=1, source_target_pairs={{0,2},{2,0},{1,3},{3,1},{4,6},{6,4},{5,7},{7,5},{8,10},{10,8},{9,1... | collective-permute-start | bytes 1032200 | tf_op jit(solution)/shard_map/ppermute | solution.py:230
  59.8 19.7 %collective-permute-start.44 = (f32[168,512]{1,0:T(8,128)S(1)}, f32[168,512]{1,0:T(8,128)S(1)}, u32[]{:S(2)}, u32[]{:S(2)}) collective-permute-start(f32[168,512]{1,0:T(8,128)S(1)} %shard_map.69.refs_0_.refs_3_), channel_id=1, source_target_pairs={{0,1},{1,0},{2,3},{3,2},{4,5},{5,4},{6,7},{7,6},{8,9},{9,8},{10,11... | collective-permute-start | bytes 1032200 | tf_op jit(solution)/shard_map/ppermute | solution.py:230
  65.7 13.9 %collective-permute-start.45 = (f32[168,512]{1,0:T(8,128)S(1)}, f32[168,512]{1,0:T(8,128)S(1)}, u32[]{:S(2)}, u32[]{:S(2)}) collective-permute-start(f32[168,512]{1,0:T(8,128)S(1)} %collective-permute-done.43.refs_1_), channel_id=1, source_target_pairs={{0,1},{1,0},{2,3},{3,2},{4,5},{5,4},{6,7},{7,6},{8,9},{9,8},{10,11... | collective-permute-start | bytes 1032200 | tf_op jit(solution)/shard_map/ppermute | solution.py:230
  74.6 16.2 %collective-permute-start.8 = (f32[168,512]{1,0:T(8,128)S(1)}, f32[168,512]{1,0:T(8,128)S(1)}, u32[]{:S(2)}, u32[]{:S(2)}) collective-permute-start(f32[168,512]{1,0:T(8,128)S(1)} %get-tuple-element.72), channel_id=1, source_target_pairs={{0,24},{8,16},{16,8},{24,0},{1,25},{9,17},{17,9},{25,1},{2,26},{10... | collective-permute-start | bytes 1032200 | tf_op jit(solution)/shard_map/ppermute | solution.py:230
  76.8 11.9 %collective-permute-start.5 = (f32[168,512]{1,0:T(8,128)S(1)}, f32[168,512]{1,0:T(8,128)S(1)}, u32[]{:S(2)}, u32[]{:S(2)}) collective-permute-start(f32[168,512]{1,0:T(8,128)S(1)} %get-tuple-element.70), channel_id=1, source_target_pairs={{0,4},{4,0},{1,5},{5,1},{2,6},{6,2},{3,7},{7,3},{8,12},{12,8},{9,1... | collective-permute-start | bytes 1032200 | tf_op jit(solution)/shard_map/ppermute | solution.py:230
  88.7 18.2 %collective-permute-start.6 = (f32[168,512]{1,0:T(8,128)S(1)}, f32[168,512]{1,0:T(8,128)S(1)}, u32[]{:S(2)}, u32[]{:S(2)}) collective-permute-start(f32[168,512]{1,0:T(8,128)S(1)} %add.158), channel_id=1, source_target_pairs={{0,8},{8,0},{16,24},{24,16},{1,9},{9,1},{17,25},{25,17},{2,10},{10... | collective-permute-start | bytes 1032200 | tf_op jit(solution)/shard_map/ppermute | solution.py:230
  90.7 30.9 %collective-permute-start.48 = (f32[168,512]{1,0:T(8,128)S(1)}, f32[168,512]{1,0:T(8,128)S(1)}, u32[]{:S(2)}, u32[]{:S(2)}) collective-permute-start(f32[168,512]{1,0:T(8,128)S(1)} %get-tuple-element.100), channel_id=1, source_target_pairs={{0,8},{8,0},{16,24},{24,16},{1,9},{9,1},{17,25},{25,17},{2,10},{10... | collective-permute-start | bytes 1032200 | tf_op jit(solution)/shard_map/ppermute | solution.py:230
  90.8 31.8 %collective-permute-start.46 = (f32[168,512]{1,0:T(8,128)S(1)}, f32[168,512]{1,0:T(8,128)S(1)}, u32[]{:S(2)}, u32[]{:S(2)}) collective-permute-start(f32[168,512]{1,0:T(8,128)S(1)} %get-tuple-element.98), channel_id=1, source_target_pairs={{0,4},{4,0},{1,5},{5,1},{2,6},{6,2},{3,7},{7,3},{8,12},{12,8},{9,1... | collective-permute-start | bytes 1032200 | tf_op jit(solution)/shard_map/ppermute | solution.py:230
  99.5 26.3 %collective-permute-start.9 = (f32[168,512]{1,0:T(8,128)S(1)}, f32[168,512]{1,0:T(8,128)S(1)}, u32[]{:S(2)}, u32[]{:S(2)}) collective-permute-start(f32[168,512]{1,0:T(8,128)S(1)} %add.160), channel_id=1, source_target_pairs={{0,4},{4,0},{1,5},{5,1},{2,6},{6,2},{3,7},{7,3},{8,12},{12,8},{9,1... | collective-permute-start | bytes 1032200 | tf_op jit(solution)/shard_map/ppermute | solution.py:230
  99.6 26.0 %collective-permute-start.51 = (f32[168,512]{1,0:T(8,128)S(1)}, f32[168,512]{1,0:T(8,128)S(1)}, u32[]{:S(2)}, u32[]{:S(2)}) collective-permute-start(f32[168,512]{1,0:T(8,128)S(1)} %add.177), channel_id=1, source_target_pairs={{0,24},{8,16},{16,8},{24,0},{1,25},{9,17},{17,9},{25,1},{2,26},{10... | collective-permute-start | bytes 1032200 | tf_op jit(solution)/shard_map/ppermute | solution.py:230
  106.9 36.9 %collective-permute-start.4 = (f32[168,512]{1,0:T(8,128)S(1)}, f32[168,512]{1,0:T(8,128)S(1)}, u32[]{:S(2)}, u32[]{:S(2)}) collective-permute-start(f32[168,512]{1,0:T(8,128)S(1)} %add.157), channel_id=1, source_target_pairs={{0,8},{8,0},{16,24},{24,16},{1,9},{9,1},{17,25},{25,17},{2,10},{10... | collective-permute-start | bytes 1032200 | tf_op jit(solution)/shard_map/ppermute | solution.py:230
  121.6 22.1 %collective-permute-start.7 = (f32[168,512]{1,0:T(8,128)S(1)}, f32[168,512]{1,0:T(8,128)S(1)}, u32[]{:S(2)}, u32[]{:S(2)}) collective-permute-start(f32[168,512]{1,0:T(8,128)S(1)} %add.159), channel_id=1, source_target_pairs={{0,24},{8,16},{16,8},{24,0},{1,25},{9,17},{17,9},{25,1},{2,26},{10... | collective-permute-start | bytes 1032200 | tf_op jit(solution)/shard_map/ppermute | solution.py:230
  122.6 24.7 %collective-permute-start.49 = (f32[168,512]{1,0:T(8,128)S(1)}, f32[168,512]{1,0:T(8,128)S(1)}, u32[]{:S(2)}, u32[]{:S(2)}) collective-permute-start(f32[168,512]{1,0:T(8,128)S(1)} %add.176), channel_id=1, source_target_pairs={{0,24},{8,16},{16,8},{24,0},{1,25},{9,17},{17,9},{25,1},{2,26},{10... | collective-permute-start | bytes 1032200 | tf_op jit(solution)/shard_map/ppermute | solution.py:230
  125.6 32.9 %collective-permute-start.47 = (f32[168,512]{1,0:T(8,128)S(1)}, f32[168,512]{1,0:T(8,128)S(1)}, u32[]{:S(2)}, u32[]{:S(2)}) collective-permute-start(f32[168,512]{1,0:T(8,128)S(1)} %add.175), channel_id=1, source_target_pairs={{0,8},{8,0},{16,24},{24,16},{1,9},{9,1},{17,25},{25,17},{2,10},{10... | collective-permute-start | bytes 1032200 | tf_op jit(solution)/shard_map/ppermute | solution.py:230
  125.8 32.7 %collective-permute-start.52 = (f32[168,512]{1,0:T(8,128)S(1)}, f32[168,512]{1,0:T(8,128)S(1)}, u32[]{:S(2)}, u32[]{:S(2)}) collective-permute-start(f32[168,512]{1,0:T(8,128)S(1)} %add.178), channel_id=1, source_target_pairs={{0,4},{4,0},{1,5},{5,1},{2,6},{6,2},{3,7},{7,3},{8,12},{12,8},{9,1... | collective-permute-start | bytes 1032200 | tf_op jit(solution)/shard_map/ppermute | solution.py:230
  144.1 15.7 %collective-permute-start.11 = (f32[168,512]{1,0:T(8,128)S(1)}, f32[168,512]{1,0:T(8,128)S(1)}, u32[]{:S(2)}, u32[]{:S(2)}) collective-permute-start(f32[168,512]{1,0:T(8,128)S(1)} %get-tuple-element.73.refs_0_.refs_4_), channel_id=1, source_target_pairs={{0,24},{8,16},{16,8},{24,0},{1,25},{9,17},{17,9},{25,1},{2,26},{10... | collective-permute-start | bytes 1032200 | tf_op jit(solution)/shard_map/ppermute | solution.py:230
  145.0 31.3 %collective-permute-start.10 = (f32[168,512]{1,0:T(8,128)S(1)}, f32[168,512]{1,0:T(8,128)S(1)}, u32[]{:S(2)}, u32[]{:S(2)}) collective-permute-start(f32[168,512]{1,0:T(8,128)S(1)} %get-tuple-element.73.refs_0_.refs_4_), channel_id=1, source_target_pairs={{0,8},{8,0},{16,24},{24,16},{1,9},{9,1},{17,25},{25,17},{2,10},{10... | collective-permute-start | bytes 1032200 | tf_op jit(solution)/shard_map/ppermute | solution.py:230
  147.3 29.0 %collective-permute-start.13 = (f32[168,512]{1,0:T(8,128)S(1)}, f32[168,512]{1,0:T(8,128)S(1)}, u32[]{:S(2)}, u32[]{:S(2)}) collective-permute-start(f32[168,512]{1,0:T(8,128)S(1)} %get-tuple-element.73.refs_0_.refs_4_), channel_id=1, source_target_pairs={{0,4},{4,0},{1,5},{5,1},{2,6},{6,2},{3,7},{7,3},{8,12},{12,8},{9,1... | collective-permute-start | bytes 1032200 | tf_op jit(solution)/shard_map/ppermute | solution.py:230
  158.8 17.5 %collective-permute-start.56 = (f32[168,512]{1,0:T(8,128)S(1)}, f32[168,512]{1,0:T(8,128)S(1)}, u32[]{:S(2)}, u32[]{:S(2)}) collective-permute-start(f32[168,512]{1,0:T(8,128)S(1)} %get-tuple-element.104.refs_0_.refs_4_), channel_id=1, source_target_pairs={{0,4},{4,0},{1,5},{5,1},{2,6},{6,2},{3,7},{7,3},{8,12},{12,8},{9,1... | collective-permute-start | bytes 1032200 | tf_op jit(solution)/shard_map/ppermute | solution.py:230
  158.9 18.4 %collective-permute-start.54 = (f32[168,512]{1,0:T(8,128)S(1)}, f32[168,512]{1,0:T(8,128)S(1)}, u32[]{:S(2)}, u32[]{:S(2)}) collective-permute-start(f32[168,512]{1,0:T(8,128)S(1)} %get-tuple-element.104.refs_0_.refs_4_), channel_id=1, source_target_pairs={{0,24},{8,16},{16,8},{24,0},{1,25},{9,17},{17,9},{25,1},{2,26},{10... | collective-permute-start | bytes 1032200 | tf_op jit(solution)/shard_map/ppermute | solution.py:230
  159.8 27.8 %collective-permute-start.12 = (f32[168,512]{1,0:T(8,128)S(1)}, f32[168,512]{1,0:T(8,128)S(1)}, u32[]{:S(2)}, u32[]{:S(2)}) collective-permute-start(f32[168,512]{1,0:T(8,128)S(1)} %collective-permute-done.11.refs_2_), channel_id=1, source_target_pairs={{0,8},{8,0},{16,24},{24,16},{1,9},{9,1},{17,25},{25,17},{2,10},{10... | collective-permute-start | bytes 1032200 | tf_op jit(solution)/shard_map/ppermute | solution.py:230
  176.3 27.3 %collective-permute-start.53 = (f32[168,512]{1,0:T(8,128)S(1)}, f32[168,512]{1,0:T(8,128)S(1)}, u32[]{:S(2)}, u32[]{:S(2)}) collective-permute-start(f32[168,512]{1,0:T(8,128)S(1)} %get-tuple-element.104.refs_0_.refs_4_), channel_id=1, source_target_pairs={{0,8},{8,0},{16,24},{24,16},{1,9},{9,1},{17,25},{25,17},{2,10},{10... | collective-permute-start | bytes 1032200 | tf_op jit(solution)/shard_map/ppermute | solution.py:230
  176.3 27.3 %collective-permute-start.14 = (f32[168,512]{1,0:T(8,128)S(1)}, f32[168,512]{1,0:T(8,128)S(1)}, u32[]{:S(2)}, u32[]{:S(2)}) collective-permute-start(f32[168,512]{1,0:T(8,128)S(1)} %collective-permute-done.10.refs_1_), channel_id=1, source_target_pairs={{0,4},{4,0},{1,5},{5,1},{2,6},{6,2},{3,7},{7,3},{8,12},{12,8},{9,1... | collective-permute-start | bytes 1032200 | tf_op jit(solution)/shard_map/ppermute | solution.py:230
  176.4 27.2 %collective-permute-start.58 = (f32[168,512]{1,0:T(8,128)S(1)}, f32[168,512]{1,0:T(8,128)S(1)}, u32[]{:S(2)}, u32[]{:S(2)}) collective-permute-start(f32[168,512]{1,0:T(8,128)S(1)} %collective-permute-done.56.refs_4_), channel_id=1, source_target_pairs={{0,24},{8,16},{16,8},{24,0},{1,25},{9,17},{17,9},{25,1},{2,26},{10... | collective-permute-start | bytes 1032200 | tf_op jit(solution)/shard_map/ppermute | solution.py:230
  177.3 31.0 %collective-permute-start.15 = (f32[168,512]{1,0:T(8,128)S(1)}, f32[168,512]{1,0:T(8,128)S(1)}, u32[]{:S(2)}, u32[]{:S(2)}) collective-permute-start(f32[168,512]{1,0:T(8,128)S(1)} %collective-permute-done.13.refs_4_), channel_id=1, source_target_pairs={{0,24},{8,16},{16,8},{24,0},{1,25},{9,17},{17,9},{25,1},{2,26},{10... | collective-permute-start | bytes 1032200 | tf_op jit(solution)/shard_map/ppermute | solution.py:230
  187.6 20.7 %collective-permute-start.16 = (f32[168,512]{1,0:T(8,128)S(1)}, f32[168,512]{1,0:T(8,128)S(1)}, u32[]{:S(2)}, u32[]{:S(2)}) collective-permute-start(f32[168,512]{1,0:T(8,128)S(1)} %collective-permute-done.12.refs_3_), channel_id=1, source_target_pairs={{0,4},{4,0},{1,5},{5,1},{2,6},{6,2},{3,7},{7,3},{8,12},{12,8},{9,1... | collective-permute-start | bytes 1032200 | tf_op jit(solution)/shard_map/ppermute | solution.py:230
  203.6 12.9 %collective-permute-start.55 = (f32[168,512]{1,0:T(8,128)S(1)}, f32[168,512]{1,0:T(8,128)S(1)}, u32[]{:S(2)}, u32[]{:S(2)}) collective-permute-start(f32[168,512]{1,0:T(8,128)S(1)} %collective-permute-done.54.refs_2_), channel_id=1, source_target_pairs={{0,8},{8,0},{16,24},{24,16},{1,9},{9,1},{17,25},{25,17},{2,10},{10... | collective-permute-start | bytes 1032200 | tf_op jit(solution)/shard_map/ppermute | solution.py:230
  203.6 12.9 %collective-permute-start.57 = (f32[168,512]{1,0:T(8,128)S(1)}, f32[168,512]{1,0:T(8,128)S(1)}, u32[]{:S(2)}, u32[]{:S(2)}) collective-permute-start(f32[168,512]{1,0:T(8,128)S(1)} %collective-permute-done.53.refs_1_), channel_id=1, source_target_pairs={{0,4},{4,0},{1,5},{5,1},{2,6},{6,2},{3,7},{7,3},{8,12},{12,8},{9,1... | collective-permute-start | bytes 1032200 | tf_op jit(solution)/shard_map/ppermute | solution.py:230
  203.6 12.9 %collective-permute-start.59 = (f32[168,512]{1,0:T(8,128)S(1)}, f32[168,512]{1,0:T(8,128)S(1)}, u32[]{:S(2)}, u32[]{:S(2)}) collective-permute-start(f32[168,512]{1,0:T(8,128)S(1)} %collective-permute-done.58.refs_6_), channel_id=1, source_target_pairs={{0,8},{8,0},{16,24},{24,16},{1,9},{9,1},{17,25},{25,17},{2,10},{10... | collective-permute-start | bytes 1032200 | tf_op jit(solution)/shard_map/ppermute | solution.py:230
  226.8 16.6 %collective-permute-start.61 = (f32[168,512]{1,0:T(8,128)S(1)}, f32[168,512]{1,0:T(8,128)S(1)}, u32[]{:S(2)}, u32[]{:S(2)}) collective-permute-start(f32[168,512]{1,0:T(8,128)S(1)} %fusion.2), channel_id=1, source_target_pairs={{0,2},{2,0},{1,3},{3,1},{4,6},{6,4},{5,7},{7,5},{8,10},{10,8},{9,1... | collective-permute-start | bytes 1032200 | tf_op jit(solution)/shard_map/ppermute | solution.py:230
  236.4 14.4 %collective-permute-start.19 = (f32[168,512]{1,0:T(8,128)S(1)}, f32[168,512]{1,0:T(8,128)S(1)}, u32[]{:S(2)}, u32[]{:S(2)}) collective-permute-start(f32[168,512]{1,0:T(8,128)S(1)} %get-tuple-element.79.refs_0_.refs_3_), channel_id=1, source_target_pairs={{0,2},{2,0},{1,3},{3,1},{4,6},{6,4},{5,7},{7,5},{8,10},{10,8},{9,1... | collective-permute-start | bytes 1032200 | tf_op jit(solution)/shard_map/ppermute | solution.py:230
  243.7 13.4 %collective-permute-start.62 = (f32[168,512]{1,0:T(8,128)S(1)}, f32[168,512]{1,0:T(8,128)S(1)}, u32[]{:S(2)}, u32[]{:S(2)}) collective-permute-start(f32[168,512]{1,0:T(8,128)S(1)} %get-tuple-element.110.refs_0_.refs_3_), channel_id=1, source_target_pairs={{0,2},{2,0},{1,3},{3,1},{4,6},{6,4},{5,7},{7,5},{8,10},{10,8},{9,1... | collective-permute-start | bytes 1032200 | tf_op jit(solution)/shard_map/ppermute | solution.py:230
  245.3 11.9 %collective-permute-start.20 = (f32[168,512]{1,0:T(8,128)S(1)}, f32[168,512]{1,0:T(8,128)S(1)}, u32[]{:S(2)}, u32[]{:S(2)}) collective-permute-start(f32[168,512]{1,0:T(8,128)S(1)} %get-tuple-element.79.refs_0_.refs_3_), channel_id=1, source_target_pairs={{0,1},{1,0},{2,3},{3,2},{4,5},{5,4},{6,7},{7,6},{8,9},{9,8},{10,11... | collective-permute-start | bytes 1032200 | tf_op jit(solution)/shard_map/ppermute | solution.py:230
  250.7 18.4 %collective-permute-start.63 = (f32[168,512]{1,0:T(8,128)S(1)}, f32[168,512]{1,0:T(8,128)S(1)}, u32[]{:S(2)}, u32[]{:S(2)}) collective-permute-start(f32[168,512]{1,0:T(8,128)S(1)} %get-tuple-element.110.refs_0_.refs_3_), channel_id=1, source_target_pairs={{0,1},{1,0},{2,3},{3,2},{4,5},{5,4},{6,7},{7,6},{8,9},{9,8},{10,11... | collective-permute-start | bytes 1032200 | tf_op jit(solution)/shard_map/ppermute | solution.py:230
  257.2 11.9 %collective-permute-start.64 = (f32[168,512]{1,0:T(8,128)S(1)}, f32[168,512]{1,0:T(8,128)S(1)}, u32[]{:S(2)}, u32[]{:S(2)}) collective-permute-start(f32[168,512]{1,0:T(8,128)S(1)} %collective-permute-done.62.refs_1_), channel_id=1, source_target_pairs={{0,1},{1,0},{2,3},{3,2},{4,5},{5,4},{6,7},{7,6},{8,9},{9,8},{10,11... | collective-permute-start | bytes 1032200 | tf_op jit(solution)/shard_map/ppermute | solution.py:230
  266.2 16.5 %collective-permute-start.27 = (f32[168,512]{1,0:T(8,128)S(1)}, f32[168,512]{1,0:T(8,128)S(1)}, u32[]{:S(2)}, u32[]{:S(2)}) collective-permute-start(f32[168,512]{1,0:T(8,128)S(1)} %get-tuple-element.87), channel_id=1, source_target_pairs={{0,24},{8,16},{16,8},{24,0},{1,25},{9,17},{17,9},{25,1},{2,26},{10... | collective-permute-start | bytes 1032200 | tf_op jit(solution)/shard_map/ppermute | solution.py:230
  278.4 13.0 %collective-permute-start.22 = (f32[168,512]{1,0:T(8,128)S(1)}, f32[168,512]{1,0:T(8,128)S(1)}, u32[]{:S(2)}, u32[]{:S(2)}) collective-permute-start(f32[168,512]{1,0:T(8,128)S(1)} %get-tuple-element.82), channel_id=1, source_target_pairs={{0,4},{4,0},{1,5},{5,1},{2,6},{6,2},{3,7},{7,3},{8,12},{12,8},{9,1... | collective-permute-start | bytes 1032200 | tf_op jit(solution)/shard_map/ppermute | solution.py:230
  280.5 16.1 %collective-permute-start.25 = (f32[168,512]{1,0:T(8,128)S(1)}, f32[168,512]{1,0:T(8,128)S(1)}, u32[]{:S(2)}, u32[]{:S(2)}) collective-permute-start(f32[168,512]{1,0:T(8,128)S(1)} %add.163), channel_id=1, source_target_pairs={{0,8},{8,0},{16,24},{24,16},{1,9},{9,1},{17,25},{25,17},{2,10},{10... | collective-permute-start | bytes 1032200 | tf_op jit(solution)/shard_map/ppermute | solution.py:230
  282.5 28.9 %collective-permute-start.67 = (f32[168,512]{1,0:T(8,128)S(1)}, f32[168,512]{1,0:T(8,128)S(1)}, u32[]{:S(2)}, u32[]{:S(2)}) collective-permute-start(f32[168,512]{1,0:T(8,128)S(1)} %get-tuple-element.115), channel_id=1, source_target_pairs={{0,8},{8,0},{16,24},{24,16},{1,9},{9,1},{17,25},{25,17},{2,10},{10... | collective-permute-start | bytes 1032200 | tf_op jit(solution)/shard_map/ppermute | solution.py:230
  282.6 28.9 %collective-permute-start.65 = (f32[168,512]{1,0:T(8,128)S(1)}, f32[168,512]{1,0:T(8,128)S(1)}, u32[]{:S(2)}, u32[]{:S(2)}) collective-permute-start(f32[168,512]{1,0:T(8,128)S(1)} %get-tuple-element.113), channel_id=1, source_target_pairs={{0,4},{4,0},{1,5},{5,1},{2,6},{6,2},{3,7},{7,3},{8,12},{12,8},{9,1... | collective-permute-start | bytes 1032200 | tf_op jit(solution)/shard_map/ppermute | solution.py:230
  289.3 26.3 %collective-permute-start.28 = (f32[168,512]{1,0:T(8,128)S(1)}, f32[168,512]{1,0:T(8,128)S(1)}, u32[]{:S(2)}, u32[]{:S(2)}) collective-permute-start(f32[168,512]{1,0:T(8,128)S(1)} %add.165), channel_id=1, source_target_pairs={{0,4},{4,0},{1,5},{5,1},{2,6},{6,2},{3,7},{7,3},{8,12},{12,8},{9,1... | collective-permute-start | bytes 1032200 | tf_op jit(solution)/shard_map/ppermute | solution.py:230
  291.4 24.0 %collective-permute-start.70 = (f32[168,512]{1,0:T(8,128)S(1)}, f32[168,512]{1,0:T(8,128)S(1)}, u32[]{:S(2)}, u32[]{:S(2)}) collective-permute-start(f32[168,512]{1,0:T(8,128)S(1)} %add.182), channel_id=1, source_target_pairs={{0,24},{8,16},{16,8},{24,0},{1,25},{9,17},{17,9},{25,1},{2,26},{10... | collective-permute-start | bytes 1032200 | tf_op jit(solution)/shard_map/ppermute | solution.py:230
  296.7 36.9 %collective-permute-start.23 = (f32[168,512]{1,0:T(8,128)S(1)}, f32[168,512]{1,0:T(8,128)S(1)}, u32[]{:S(2)}, u32[]{:S(2)}) collective-permute-start(f32[168,512]{1,0:T(8,128)S(1)} %add.162), channel_id=1, source_target_pairs={{0,8},{8,0},{16,24},{24,16},{1,9},{9,1},{17,25},{25,17},{2,10},{10... | collective-permute-start | bytes 1032200 | tf_op jit(solution)/shard_map/ppermute | solution.py:230
  311.4 22.1 %collective-permute-start.26 = (f32[168,512]{1,0:T(8,128)S(1)}, f32[168,512]{1,0:T(8,128)S(1)}, u32[]{:S(2)}, u32[]{:S(2)}) collective-permute-start(f32[168,512]{1,0:T(8,128)S(1)} %add.164), channel_id=1, source_target_pairs={{0,24},{8,16},{16,8},{24,0},{1,25},{9,17},{17,9},{25,1},{2,26},{10... | collective-permute-start | bytes 1032200 | tf_op jit(solution)/shard_map/ppermute | solution.py:230
  311.5 25.7 %collective-permute-start.68 = (f32[168,512]{1,0:T(8,128)S(1)}, f32[168,512]{1,0:T(8,128)S(1)}, u32[]{:S(2)}, u32[]{:S(2)}) collective-permute-start(f32[168,512]{1,0:T(8,128)S(1)} %add.181), channel_id=1, source_target_pairs={{0,24},{8,16},{16,8},{24,0},{1,25},{9,17},{17,9},{25,1},{2,26},{10... | collective-permute-start | bytes 1032200 | tf_op jit(solution)/shard_map/ppermute | solution.py:230
  315.4 32.9 %collective-permute-start.66 = (f32[168,512]{1,0:T(8,128)S(1)}, f32[168,512]{1,0:T(8,128)S(1)}, u32[]{:S(2)}, u32[]{:S(2)}) collective-permute-start(f32[168,512]{1,0:T(8,128)S(1)} %add.180), channel_id=1, source_target_pairs={{0,8},{8,0},{16,24},{24,16},{1,9},{9,1},{17,25},{25,17},{2,10},{10... | collective-permute-start | bytes 1032200 | tf_op jit(solution)/shard_map/ppermute | solution.py:230
  315.6 32.7 %collective-permute-start.71 = (f32[168,512]{1,0:T(8,128)S(1)}, f32[168,512]{1,0:T(8,128)S(1)}, u32[]{:S(2)}, u32[]{:S(2)}) collective-permute-start(f32[168,512]{1,0:T(8,128)S(1)} %add.183), channel_id=1, source_target_pairs={{0,4},{4,0},{1,5},{5,1},{2,6},{6,2},{3,7},{7,3},{8,12},{12,8},{9,1... | collective-permute-start | bytes 1032200 | tf_op jit(solution)/shard_map/ppermute | solution.py:230
  334.0 16.8 %collective-permute-start.30 = (f32[168,512]{1,0:T(8,128)S(1)}, f32[168,512]{1,0:T(8,128)S(1)}, u32[]{:S(2)}, u32[]{:S(2)}) collective-permute-start(f32[168,512]{1,0:T(8,128)S(1)} %get-tuple-element.89.refs_0_), channel_id=1, source_target_pairs={{0,24},{8,16},{16,8},{24,0},{1,25},{9,17},{17,9},{25,1},{2,26},{10... | collective-permute-start | bytes 1032200 | tf_op jit(solution)/shard_map/ppermute | solution.py:230
  334.0 32.0 %collective-permute-start.29 = (f32[168,512]{1,0:T(8,128)S(1)}, f32[168,512]{1,0:T(8,128)S(1)}, u32[]{:S(2)}, u32[]{:S(2)}) collective-permute-start(f32[168,512]{1,0:T(8,128)S(1)} %get-tuple-element.89.refs_0_), channel_id=1, source_target_pairs={{0,8},{8,0},{16,24},{24,16},{1,9},{9,1},{17,25},{25,17},{2,10},{10... | collective-permute-start | bytes 1032200 | tf_op jit(solution)/shard_map/ppermute | solution.py:230
  337.1 29.0 %collective-permute-start.32 = (f32[168,512]{1,0:T(8,128)S(1)}, f32[168,512]{1,0:T(8,128)S(1)}, u32[]{:S(2)}, u32[]{:S(2)}) collective-permute-start(f32[168,512]{1,0:T(8,128)S(1)} %get-tuple-element.89.refs_0_), channel_id=1, source_target_pairs={{0,4},{4,0},{1,5},{5,1},{2,6},{6,2},{3,7},{7,3},{8,12},{12,8},{9,1... | collective-permute-start | bytes 1032200 | tf_op jit(solution)/shard_map/ppermute | solution.py:230
  348.7 19.6 %collective-permute-start.75 = (f32[168,512]{1,0:T(8,128)S(1)}, f32[168,512]{1,0:T(8,128)S(1)}, u32[]{:S(2)}, u32[]{:S(2)}) collective-permute-start(f32[168,512]{1,0:T(8,128)S(1)} %get-tuple-element.120.refs_0_), channel_id=1, source_target_pairs={{0,4},{4,0},{1,5},{5,1},{2,6},{6,2},{3,7},{7,3},{8,12},{12,8},{9,1... | collective-permute-start | bytes 1032200 | tf_op jit(solution)/shard_map/ppermute | solution.py:230
  350.8 18.4 %collective-permute-start.73 = (f32[168,512]{1,0:T(8,128)S(1)}, f32[168,512]{1,0:T(8,128)S(1)}, u32[]{:S(2)}, u32[]{:S(2)}) collective-permute-start(f32[168,512]{1,0:T(8,128)S(1)} %get-tuple-element.120.refs_0_), channel_id=1, source_target_pairs={{0,24},{8,16},{16,8},{24,0},{1,25},{9,17},{17,9},{25,1},{2,26},{10... | collective-permute-start | bytes 1032200 | tf_op jit(solution)/shard_map/ppermute | solution.py:230
  350.8 26.8 %collective-permute-start.31 = (f32[168,512]{1,0:T(8,128)S(1)}, f32[168,512]{1,0:T(8,128)S(1)}, u32[]{:S(2)}, u32[]{:S(2)}) collective-permute-start(f32[168,512]{1,0:T(8,128)S(1)} %collective-permute-done.30.refs_2_), channel_id=1, source_target_pairs={{0,8},{8,0},{16,24},{24,16},{1,9},{9,1},{17,25},{25,17},{2,10},{10... | collective-permute-start | bytes 1032200 | tf_op jit(solution)/shard_map/ppermute | solution.py:230
  366.1 27.3 %collective-permute-start.72 = (f32[168,512]{1,0:T(8,128)S(1)}, f32[168,512]{1,0:T(8,128)S(1)}, u32[]{:S(2)}, u32[]{:S(2)}) collective-permute-start(f32[168,512]{1,0:T(8,128)S(1)} %get-tuple-element.120.refs_0_), channel_id=1, source_target_pairs={{0,8},{8,0},{16,24},{24,16},{1,9},{9,1},{17,25},{25,17},{2,10},{10... | collective-permute-start | bytes 1032200 | tf_op jit(solution)/shard_map/ppermute | solution.py:230
  366.1 27.3 %collective-permute-start.33 = (f32[168,512]{1,0:T(8,128)S(1)}, f32[168,512]{1,0:T(8,128)S(1)}, u32[]{:S(2)}, u32[]{:S(2)}) collective-permute-start(f32[168,512]{1,0:T(8,128)S(1)} %collective-permute-done.29.refs_1_), channel_id=1, source_target_pairs={{0,4},{4,0},{1,5},{5,1},{2,6},{6,2},{3,7},{7,3},{8,12},{12,8},{9,1... | collective-permute-start | bytes 1032200 | tf_op jit(solution)/shard_map/ppermute | solution.py:230
  368.3 27.3 %collective-permute-start.77 = (f32[168,512]{1,0:T(8,128)S(1)}, f32[168,512]{1,0:T(8,128)S(1)}, u32[]{:S(2)}, u32[]{:S(2)}) collective-permute-start(f32[168,512]{1,0:T(8,128)S(1)} %collective-permute-done.75.refs_4_), channel_id=1, source_target_pairs={{0,24},{8,16},{16,8},{24,0},{1,25},{9,17},{17,9},{25,1},{2,26},{10... | collective-permute-start | bytes 1032200 | tf_op jit(solution)/shard_map/ppermute | solution.py:230
  369.2 28.9 %collective-permute-start.34 = (f32[168,512]{1,0:T(8,128)S(1)}, f32[168,512]{1,0:T(8,128)S(1)}, u32[]{:S(2)}, u32[]{:S(2)}) collective-permute-start(f32[168,512]{1,0:T(8,128)S(1)} %collective-permute-done.32.refs_4_), channel_id=1, source_target_pairs={{0,24},{8,16},{16,8},{24,0},{1,25},{9,17},{17,9},{25,1},{2,26},{10... | collective-permute-start | bytes 1032200 | tf_op jit(solution)/shard_map/ppermute | solution.py:230
  377.6 20.5 %collective-permute-start.35 = (f32[168,512]{1,0:T(8,128)S(1)}, f32[168,512]{1,0:T(8,128)S(1)}, u32[]{:S(2)}, u32[]{:S(2)}) collective-permute-start(f32[168,512]{1,0:T(8,128)S(1)} %collective-permute-done.31.refs_3_), channel_id=1, source_target_pairs={{0,4},{4,0},{1,5},{5,1},{2,6},{6,2},{3,7},{7,3},{8,12},{12,8},{9,1... | collective-permute-start | bytes 1032200 | tf_op jit(solution)/shard_map/ppermute | solution.py:230
  393.4 12.7 %collective-permute-start.74 = (f32[168,512]{1,0:T(8,128)S(1)}, f32[168,512]{1,0:T(8,128)S(1)}, u32[]{:S(2)}, u32[]{:S(2)}) collective-permute-start(f32[168,512]{1,0:T(8,128)S(1)} %collective-permute-done.73.refs_2_), channel_id=1, source_target_pairs={{0,8},{8,0},{16,24},{24,16},{1,9},{9,1},{17,25},{25,17},{2,10},{10... | collective-permute-start | bytes 1032200 | tf_op jit(solution)/shard_map/ppermute | solution.py:230
  393.4 12.7 %collective-permute-start.76 = (f32[168,512]{1,0:T(8,128)S(1)}, f32[168,512]{1,0:T(8,128)S(1)}, u32[]{:S(2)}, u32[]{:S(2)}) collective-permute-start(f32[168,512]{1,0:T(8,128)S(1)} %collective-permute-done.72.refs_1_), channel_id=1, source_target_pairs={{0,4},{4,0},{1,5},{5,1},{2,6},{6,2},{3,7},{7,3},{8,12},{12,8},{9,1... | collective-permute-start | bytes 1032200 | tf_op jit(solution)/shard_map/ppermute | solution.py:230
  416.7 15.8 %collective-permute-start.80 = (f32[168,512]{1,0:T(8,128)S(1)}, f32[168,512]{1,0:T(8,128)S(1)}, u32[]{:S(2)}, u32[]{:S(2)}) collective-permute-start(f32[168,512]{1,0:T(8,128)S(1)} %fusion.1), channel_id=1, source_target_pairs={{0,2},{2,0},{1,3},{3,1},{4,6},{6,4},{5,7},{7,5},{8,10},{10,8},{9,1... | collective-permute-start | bytes 1032200 | tf_op jit(solution)/shard_map/ppermute | solution.py:230
  442.0 22.7 %collective-permute-start.84 = (f32[8,128]{1,0:T(8,128)S(1)}, f32[8,128]{1,0:T(8,128)S(1)}, u32[]{:S(2)}, u32[]{:S(2)}) collective-permute-start(f32[8,128]{1,0:T(8,128)S(1)} %add.188), channel_id=1, source_target_pairs={{0,8},{8,0},{16,24},{24,16},{1,9},{9,1},{17,25},{25,17},{2,10},{10... | collective-permute-start | bytes 12296 | tf_op jit(solution)/shard_map/ppermute | solution.py:230
  443.8 22.2 %collective-permute-start.42 = (f32[8,128]{1,0:T(8,128)S(1)}, f32[8,128]{1,0:T(8,128)S(1)}, u32[]{:S(2)}, u32[]{:S(2)}) collective-permute-start(f32[8,128]{1,0:T(8,128)S(1)} %add.171), channel_id=1, source_target_pairs={{0,24},{8,16},{16,8},{24,0},{1,25},{9,17},{17,9},{25,1},{2,26},{10... | collective-permute-start | bytes 12296 | tf_op jit(solution)/shard_map/ppermute | solution.py:230
  (23 other events, 158.3 us)

commit v2 on v1

--- a/solution.py
+++ b/solution.py
@@ -39,15 +39,9 @@
     return total
 
 
-def xor_index(axis, k):
+def other(axis):
     index = lax.axis_index(axis)
-    if k == 0:
-        return index
-    if k == 1:
-        return index + 1 - 2 * lax.rem(index, 2)
-    if k == 3:
-        return 3 - index
-    return lax.rem(index + 2, 4)
+    return index + 1 - 2 * lax.rem(index, 2)
 
 
 def product_kernel(adjoint, places, outs, k_ref, *refs):
@@ -219,10 +213,7 @@
         out_shape=jax.ShapeDtypeStruct((row_count + HEAD, width), jnp.float32),
         compiler_params=params,
     )
-    first = exchange(first)
-    marks = first[:, width:]
-    second = exchange(second)
-    return [unpack(first, marks), unpack(second, marks)]
+    return [first, second], exchange, unpack
 
 
 def swap(values, axis, k=1):
@@ -230,52 +221,108 @@
     return lax.ppermute(values, axis, [(i, i ^ k) for i in range(size)])
 
 
-def rec_place(kz, ky):
-    return lambda: xor_index("z", kz) * 2 + xor_index("y", ky)
-
-
-def src_place(kx, kc):
-    return lambda: xor_index("x", kx) * 2 + xor_index("c", kc)
+def at_end():
+    index = lax.axis_index("z")
+    return (index == 0) | (index == 3)
+
+
+ASKED = {
+    "y": lambda values: swap(values, "y"),
+    "x": lambda values: swap(values, "x"),
+    "c": lambda values: swap(values, "c"),
+    "z": lambda values: swap(values, "z"),
+    "mid": lambda values: lax.ppermute(values, "z", [(1, 2), (2, 1)]),
+    "up": lambda values: lax.ppermute(values, "z", [(0, 1), (3, 2)]),
+    "down": lambda values: lax.ppermute(values, "z", [(1, 0), (2, 3)]),
+    "hold": lambda values: values,
+}
+
+
+def answer(asked):
+    results = [None] * len(asked)
+    kinds = [kind for kind, _ in asked]
+    if "up" in kinds and "down" in kinds:
+        up, down = kinds.index("up"), kinds.index("down")
+        both = jnp.where(at_end(), asked[up][1], asked[down][1])
+        results[up] = results[down] = swap(both, "z")
+    for kind in ASKED:
+        for index, (wanted, values) in enumerate(asked):
+            if wanted == kind and results[index] is None:
+                results[index] = ASKED[kind](values)
+    for index, (wanted, values) in enumerate(asked):
+        if results[index] is None:
+            results[index] = swap(values, *wanted)
+    return results
+
+
+def line_place(kind):
+    index = lax.axis_index("z")
+    if kind == "own":
+        return index
+    if kind == "partner":
+        return other("z")
+    near = jnp.where(index < 2, 1, 0)
+    return 1 + near if kind == "third" else 3 * near
+
+
+def rec_place(kind, across):
+    return lambda: line_place(kind) * 2 + (other("y") if across else lax.axis_index("y"))
+
+
+def src_place(across_x, across_c):
+    return lambda: (other("x") if across_x else lax.axis_index("x")) * 2 + (
+        other("c") if across_c else lax.axis_index("c")
+    )
+
+
+KINDS = ("own", "partner", "third", "far")
 
 
 class Neighbours:
-    def gather_src(self, piece, slab):
-        x = swap(piece, "x")
-        c = swap(piece, "c")
-        xc = swap(x, "c")
-        return [piece, x, c, xc], [src_place(*k) for k in ((0, 0), (1, 0), (0, 1), (1, 1))]
-
-    def gather_rec(self, piece, slab):
-        one, three, side = swap(piece, "z", 1), swap(piece, "z", 3), swap(piece, "y")
-        two = swap(three, "z", 1)
-        side_three = swap(side, "z", 3)
-        side_one = swap(one, "y")
-        side_two = swap(two, "y") if slab == 0 else swap(side_three, "z", 1)
-        order = ((0, 0), (1, 0), (3, 0), (2, 0), (0, 1), (1, 1), (3, 1), (2, 1))
-        return [piece, one, three, two, side, side_one, side_three, side_two], [
-            rec_place(*k) for k in order
+    rec_outs = [[rec_place(kind, across)] for across in (0, 1) for kind in KINDS]
+    src_outs = [[src_place(0, 1), src_place(1, 1)], [src_place(1, 0)], [src_place(0, 0)]]
+
+    def gather_src(self, own):
+        x, c = yield ("x", own), ("c", own)
+        return [own, x, c, swap(x, "c")], [src_place(*k) for k in ((0, 0), (1, 0), (0, 1), (1, 1))]
+
+    def gather_rec(self, own):
+        own_y, partner, mid = yield ("y", own), ("z", own), ("mid", own)
+        third, mid_two, own_y = yield ("down", mid), ("mid", partner), ("hold", own_y)
+        third = jnp.where(at_end(), third, mid)
+        third_y, far, own_y = yield ("y", third), ("down", mid_two), ("hold", own_y)
+        far = jnp.where(at_end(), far, mid_two)
+        far_y, partner_y, third_y = yield ("y", far), ("z", own_y), ("hold", third_y)
+        return [own, partner, third, far, own_y, partner_y, third_y, far_y], [
+            place for (place,) in self.rec_outs
         ]
 
-    rec_outs = [[rec_place(*k)] for k in ((2, 1), (3, 1), (1, 1), (2, 0))] + [
-        [rec_place(*k)] for k in ((0, 0), (1, 0), (3, 0), (0, 1))
-    ]
-    src_outs = [[src_place(0, 1), src_place(1, 1)], [src_place(1, 0)], [src_place(0, 0)]]
-
-    def scatter_rec(self, blocks, slab):
-        side_two, side_three, side_one, two, own, one, three, side = blocks
-        if slab == 0:
-            two = two + swap(side_two, "y")
-        else:
-            side_three = side_three + swap(side_two, "z", 1)
-        one = one + swap(side_one, "y")
-        side = side + swap(side_three, "z", 3)
-        three = three + swap(two, "z", 1)
-        return [own, swap(one, "z", 1), swap(three, "z", 3), swap(side, "y")]
-
-    def scatter_src(self, blocks, slab):
-        sent, across, own = blocks
+    def scatter_rec(self, blocks):
+        blocks = yield tuple(("hold", block) for block in blocks)
+        own, partner, third, far, own_y, partner_y, third_y, far_y = blocks
+        got_far, got_own_y, third_y, own_y, third = yield (
+            ("y", far_y), ("z", partner_y), ("hold", third_y), ("hold", own_y), ("hold", third),
+        )
+        own_y = own_y + got_own_y
+        far = far + got_far
+        got_third, got_far, own_y, third, far = yield (
+            ("y", third_y), ("up", far), ("hold", own_y), ("hold", third), ("hold", far),
+        )
+        third = third + got_third
+        far = far + got_far
+        got_third, got_partner, own_y, third = yield (
+            ("up", third), ("mid", far), ("hold", own_y), ("hold", third),
+        )
+        partner = partner + got_partner
+        third = third + got_third
+        last = yield ("y", own_y), ("z", partner), ("mid", third)
+        return [own, *last]
+
+    def scatter_src(self, blocks):
+        sent, across, own = yield tuple(("hold", block) for block in blocks)
         back = swap(sent, "c")
-        return [own, back[0], swap(across + back[1], "x")]
+        (far,) = yield (("x", across + back[1]),)
+        return [own, back[0], far]
 
 
 class Whole:
@@ -295,16 +342,20 @@
         both = jnp.concatenate([head, data], axis=1)
         return [lax.psum_scatter(both, axes, scatter_dimension=0, tiled=False)]
 
-    def gather_src(self, piece, slab):
+    def gather_src(self, piece):
+        (piece,) = yield (("hold", piece),)
         return self.gather(piece, SRC)
 
-    def gather_rec(self, piece, slab):
+    def gather_rec(self, piece):
+        (piece,) = yield (("hold", piece),)
         return self.gather(piece, REC)
 
-    def scatter_rec(self, blocks, slab):
+    def scatter_rec(self, blocks):
+        (blocks,) = yield (("hold", blocks),)
         return self.scatter(blocks, REC)
 
-    def scatter_src(self, blocks, slab):
+    def scatter_src(self, blocks):
+        (blocks,) = yield (("hold", blocks),)
         return self.scatter(blocks, SRC)
 
 
@@ -312,9 +363,115 @@
     for axis in ("c", "x", "y", "z"):
         k = 1
         while k < lax.axis_size(axis):
-            values = values + swap(values, axis, 2 * k - 1)
+            (got,) = yield (((axis, 2 * k - 1), values),)
+            values = values + got
             k *= 2
     return values
+
+
+LAG = 4
+
+
+def in_slots(chains, lag):
+    values, results, slot = [None] * len(chains), [None] * len(chains), 0
+    live = list(range(len(chains)))
+    while live:
+        made = {}
+        for index in list(live):
+            if slot < index * lag:
+                continue
+            try:
+                made[index] = chains[index].send(values[index])
+            except StopIteration as stop:
+                results[index] = stop.value
+                live.remove(index)
+        asked = [request for requests in made.values() for request in requests]
+        given = iter(lax.optimization_barrier(tuple(answer(asked))))
+        for index, requests in made.items():
+            values[index] = tuple(next(given) for _ in requests)
+        slot += 1
+    return results
+
+
+def chain(moves, kernel, slab, packed, shared, exchange, unpack, row_count, column_count, count):
+    def adjoint(piece):
+        pieces, places = yield from moves.gather_src(piece)
+        rows = column_count if len(moves.rec_outs) > 1 else kernel.shape[3]
+        blocks = product(kernel, slab, True, pieces, places, moves.rec_outs, rows)
+        return (yield from moves.scatter_rec(blocks))
+
+    def forward(piece):
+        pieces, places = yield from moves.gather_rec(piece)
+        rows = row_count if len(moves.src_outs) > 1 else kernel.shape[2]
+        blocks = product(kernel, slab, False, pieces, places, moves.src_outs, rows)
+        return (yield from moves.scatter_src(blocks))
+
+    (packed,) = yield (("hold", packed),)
+    (packed,) = yield (("hold", exchange(packed)),)
+    if slab == 0:
+        shared["marks"] = packed[:, 2 * SOURCES :]
+    left = unpack(packed, shared["marks"])
+    right, beta = finish(count, (yield from adjoint(left)))
+    rights, norms = [], [beta]
+    for iteration in range(ITERS):
+        left, alpha = finish(count, (yield from forward(right)), left, beta)
+        rights.append(right)
+        norms.append(alpha)
+        if iteration + 1 < ITERS:
+            right, beta = finish(count, (yield from adjoint(left)), right, alpha)
+            norms.append(beta)
+    norms.append((yield from global_sum(left[:HEAD, :128])))
+    return rights, norms, left
+
+
+def join_left_kernel(*refs):
+    out = refs[-1]
+    half = refs[0].shape[1] // 2
+    for slab, left in enumerate(refs[:-1]):
+        for part in range(2):
+            at = (part * FREQS + slab) * half
+            out[:, at : at + half] = left[HEAD:, part * half : (part + 1) * half]
+
+
+def join_solution_kernel(count, *refs):
+    refs, out = refs[:-1], refs[-1]
+    half = refs[0].shape[1] // 2
+    for slab in range(FREQS):
+        start = slab * (3 * ITERS + 1)
+        rights = refs[start : start + ITERS]
+        norms = [ref[:1, :1] for ref in refs[start + ITERS : start + 3 * ITERS + 1]]
+        norms[-1] = jnp.sqrt(norms[-1] / count)
+        phibar, betas, alphas = norms[0], norms[2::2], norms[1::2]
+        for iteration in range(ITERS):
+            unit = rights[iteration][HEAD:, :] / alphas[iteration]
+            if iteration == 0:
+                rhobar, search = alphas[0], unit
+            else:
+                rhobar = -cosine * alphas[iteration]
+                search = unit - (sine * alphas[iteration] / rho) * search
+            rho = jnp.sqrt(rhobar * rhobar + betas[iteration] * betas[iteration])
+            cosine = rhobar / rho
+            sine = betas[iteration] / rho
+            phi = cosine * phibar
+            phibar = sine * phibar
+            step = (phi / rho) * search
+            solution = step if iteration == 0 else solution + step
+        for part in range(2):
+            at = (part * FREQS + slab) * half
+            out[:, at : at + half] = solution[:, part * half : (part + 1) * half]
+
+
+def join(kernel, pieces):
+    rows, width = pieces[0].shape[0] - HEAD, pieces[0].shape[1] * FREQS
+    joined = pl.pallas_call(
+        kernel,
+        out_shape=jax.ShapeDtypeStruct((rows, width), jnp.float32),
+        compiler_params=pltpu.CompilerParams(vmem_limit_bytes=VMEM_BYTES),
+        cost_estimate=pl.CostEstimate(
+            flops=rows * width * 4, bytes_accessed=8 * rows * width, transcendentals=0
+        ),
+    )(*pieces)
+    return joined.reshape(rows, 2, FREQS, SOURCES)
 
 
 def on_device(kernel, traces, acq_lists, counts):
@@ -324,54 +481,20 @@
     aligned = row_count % 16 == 0 and column_count % 16 == 0
     moves = Neighbours() if sizes == (4, 2, 2, 2) and aligned else Whole()
     count = 2.0 * kernel.shape[2] * sizes[0] * sizes[1] * SOURCES
-
-    def adjoint(piece, slab):
-        pieces, places = moves.gather_src(piece, slab)
-        rows = column_count if len(moves.rec_outs) > 1 else kernel.shape[3]
-        blocks = product(kernel, slab, True, pieces, places, moves.rec_outs, rows)
-        return moves.scatter_rec(blocks, slab)
-
-    def forward(piece, slab):
-        pieces, places = moves.gather_rec(piece, slab)
-        rows = row_count if len(moves.src_outs) > 1 else kernel.shape[2]
-        blocks = product(kernel, slab, False, pieces, places, moves.src_outs, rows)
-        return moves.scatter_src(blocks, slab)
-
-    observed = dispatch(traces, acq_lists, counts, row_count)
-    solutions, lefts = [], []
-    for slab in range(FREQS):
-        left = observed[slab]
-        right, beta = finish(count, adjoint(left, slab))
-        phibar = beta[0, 0]
-        search = None
-        for iteration in range(ITERS):
-            left, alpha = finish(count, forward(right, slab), left, beta)
-            unit = right[HEAD:] / alpha[0, 0]
-            if iteration == 0:
-                rhobar = alpha[0, 0]
-                search = unit
-            else:
-                rhobar = -cosine * alpha[0, 0]
-                search = unit - (sine * alpha[0, 0] / rho) * search
-            if iteration + 1 < ITERS:
-                right, beta = finish(count, adjoint(left, slab), right, alpha)
-                beta_norm = beta[0, 0]
-            else:
-                beta_norm = jnp.sqrt(global_sum(left[:HEAD, :128])[0, 0] / count)
-            rho = jnp.sqrt(rhobar * rhobar + beta_norm * beta_norm)
-            cosine = rhobar / rho
-            sine = beta_norm / rho
-            phi = cosine * phibar
-            phibar = sine * phibar
-            step = (phi / rho) * search
-            solution = step if iteration == 0 else solution + step
-        solutions.append(solution)
-        lefts.append(left[HEAD:])
-
-    def joined(parts):
-        return jnp.stack([p.reshape(p.shape[0], 2, SOURCES) for p in parts], axis=2)
-
-    return joined(solutions), joined(lefts)
+    shared = {}
+    packed, exchange, unpack = dispatch(traces, acq_lists, counts, row_count)
+    chains = [
+        chain(
+            moves, kernel, slab, packed[slab], shared, exchange, unpack,
+            row_count, column_count, count,
+        )
+        for slab in range(FREQS)
+    ]
+    rights, norms, lefts = zip(*in_slots(chains, LAG))
+    given = [ref for pair in zip(rights, norms) for group in pair for ref in group]
+    return join(functools.partial(join_solution_kernel, count), given), join(
+        join_left_kernel, lefts
+    )
 
 
 def solution(mesh):

time: 480 us -> 461 us (0.960)
  between operations: 17.2 us -> 2.58 us
  waiting for transfers between devices: 216 us -> 209 us
    ppermute x0 -> x24, waiting for transfers between devices: none -> 54.7 us  [the longest x4 28.8 us: lax.ppermute(values, 'z', [(1, 0), (2, 3)])]
    ppermute x86 -> x74, waiting for transfers between devices: 202 us -> 155 us  [swap(): return lax.ppermute(values, axis, [(i, i ^ k) for i in range(size)])]
    ppermute x86 -> x74, starting transfers between devices: 119 us -> 82.5 us  [swap(): return lax.ppermute(values, axis, [(i, i ^ k) for i in range(size)])]
    ppermute x0 -> x24, starting transfers between devices: none -> 35.6 us  [the longest x4 17.9 us: lax.ppermute(values, 'z', [(0, 1), (3, 2)])]
    all_to_all x1, waiting for transfers between devices: 14.2 us -> 0.01 us  [exchange(): packed = lax.all_to_all(packed, REC, 0, 0, tiled=True)]
    slice x15 -> x3, local copies, waits for them, and re-layouts: 5.5 us -> 0.02 us  [the longest x1 0.01 us: chain(): shared['marks'] = packed[:, 2 * SOURCES:]]
  transfers between devices with their start and end apart: 87 -> 99, of which waited for: 32 -> 58; matrix products, arithmetic and copies ran while one was open for 2% -> 2% of each run, Pallas kernels for 15% -> 13%
where the time goes in v2:
time: 461 us; the launch traced here: 454 us
  waiting for transfers between devices  209 us (45%)
  starting transfers between devices  122 us (26%)
  Pallas kernels  75.2 us (16%)
  blocking collectives  28.7 us (6%)
  other arithmetic  9.43 us (2%)
  local copies, waits for them, and re-layouts  7.18 us (2%)
    ppermute x74, waiting for transfers between devices, swap(): return lax.ppermute(values, axis, [(i, i ^ k) for i in range(size)])  155 us
    ppermute x74, starting transfers between devices, swap(): return lax.ppermute(values, axis, [(i, i ^ k) for i in range(size)])  82.5 us
    pallas_call x8, Pallas kernels, product(): pl.pallas_call(functools.partial(product_kernel, adjoint, places, outs),...  68.2 us
    ppermute x4, waiting for transfers between devices, lax.ppermute(values, 'z', [(1, 0), (2, 3)])  28.8 us
    all_to_all x1, blocking collectives, exchange(): packed = lax.all_to_all(packed, REC, 0, 0, tiled=True)  28.7 us
    ppermute x4, waiting for transfers between devices, lax.ppermute(values, 'z', [(0, 1), (3, 2)])  25.9 us
    ppermute x4, starting transfers between devices, lax.ppermute(values, 'z', [(0, 1), (3, 2)])  17.9 us
    ppermute x16, starting transfers between devices, lax.ppermute(values, 'z', [(1, 2), (2, 1)])  12.3 us
  transfers between devices with their start and end apart: 99, of which 58 were waited for; matrix products, arithmetic and copies ran while one was open for 2% of the time, Pallas kernels for 13%

profile of v2, /device:TPU:0, one launch (start us, length us, event | category | flops | bytes accessed | tf_op | source)
XLA Modules:
  0.0 453.9 jit_solution(15020140787466941454)
XLA Ops:
  3.2 2.3 reshape.149.traces_ref
  5.9 2.2 shard_map.59
  8.1 28.7 %all_to_all.10 = f32[8,40,640]{2,1,0:T(8,128)S(1)} all-to-all(f32[8,40,640]{2,1,0:T(8,128)S(1)} %bitcast.40), channel_id=1, replica_groups=mesh['z'=4,'y'=2,'x'=2,'c'=2] {'z','y'}, dimensions={0} | all-to-all | bytes 1638400 | tf_op jit(solution)/shard_map/all_to_all | solution.py:208
  39.2 8.8 %collective-permute-done.refs_1_ = f32[168,512]{1,0:T(8,128)S(1)} collective-permute-done((f32[168,512]{1,0:T(8,128)S(1)}, f32[168,512]{1,0:T(8,128)S(1)}, u32[]{:S(2)}, u32[]{:S(2)}) %collective-permute-start) | collective-permute-done | bytes 344096 | tf_op jit(solution)/shard_map/ppermute | solution.py:221
  49.7 8.9 %shard_map.61 = (f32[168,512]{1,0:T(8,128)S(1)}, f32[168,512]{1,0:T(8,128)S(1)}, f32[168,512]{1,0:T(8,128)S(1)}, f32[168,512]{1,0:T(8,128)S(1)}, f32[168,512]{1,...) custom-call(f32[2,2,640,1280]{3,2,1,0:T(8,128)} %k_ref.15, ...), custom_call_target="tpu_custom_call" | custom-call | flops 5033164800 | bytes 10485760 | tf_op jit(solution)/shard_map/pallas_call | solution.py:103
  59.9 8.9 %collective-permute-done.3 = f32[168,512]{1,0:T(8,128)S(1)} collective-permute-done((f32[168,512]{1,0:T(8,128)S(1)}, f32[168,512]{1,0:T(8,128)S(1)}, u32[]{:S(2)}, u32[]{:S(2)}) %collective-permute-start.3) | collective-permute-done | bytes 344096 | tf_op jit(solution)/shard_map/ppermute | solution.py:221
  70.0 3.5 all-to-all-start.1
  74.6 3.9 collective-permute-start.6
  81.7 9.3 %collective-permute-done.6 = f32[168,512]{1,0:T(8,128)S(1)} collective-permute-done((f32[168,512]{1,0:T(8,128)S(1)}, f32[168,512]{1,0:T(8,128)S(1)}, u32[]{:S(2)}, u32[]{:S(2)}) %collective-permute-start.6) | collective-permute-done | bytes 344096 | tf_op jit(solution)/shard_map/ppermute | solution.py:235
  96.1 8.2 %collective-permute-start.7 = (f32[168,512]{1,0:T(8,128)S(1)}, f32[168,512]{1,0:T(8,128)S(1)}, u32[]{:S(2)}, u32[]{:S(2)}) collective-permute-start(f32[168,512]{1,0:T(8,128)S(1)} %add.165), channel_id=1, source_target_pairs={{0,8},{24,16},{1,9},{25,17},{2,10},{26,18},{3,11},{27,19},{4,12},{... | collective-permute-start | bytes 1032200 | tf_op jit(solution)/shard_map/ppermute | solution.py:235
  104.4 7.3 %collective-permute-done.7 = f32[168,512]{1,0:T(8,128)S(1)} collective-permute-done((f32[168,512]{1,0:T(8,128)S(1)}, f32[168,512]{1,0:T(8,128)S(1)}, u32[]{:S(2)}, u32[]{:S(2)}) %collective-permute-start.7) | collective-permute-done | bytes 344096 | tf_op jit(solution)/shard_map/ppermute | solution.py:235
  112.6 4.1 collective-permute-start.12
  118.2 9.8 %shard_map.63 = (f32[168,512]{1,0:T(8,128)S(1)}, f32[168,512]{1,0:T(8,128)S(1)}, f32[168,512]{1,0:T(8,128)S(1)}, f32[168,512]{1,0:T(8,128)S(1)}, f32[168,512]{1,...) custom-call(f32[2,2,640,1280]{3,2,1,0:T(8,128)} %k_ref.15, ...), custom_call_target="tpu_custom_call" | custom-call | flops 5033164800 | bytes 10485760 | tf_op jit(solution)/shard_map/pallas_call | solution.py:103
  129.8 2.4 collective-permute-start.16
  134.3 6.8 %collective-permute-done.16.refs_1_ = f32[168,512]{1,0:T(8,128)S(1)} collective-permute-done((f32[168,512]{1,0:T(8,128)S(1)}, f32[168,512]{1,0:T(8,128)S(1)}, u32[]{:S(2)}, u32[]{:S(2)}) %collective-permute-start.16) | collective-permute-done | bytes 344096 | tf_op jit(solution)/shard_map/ppermute | solution.py:221
  141.1 2.2 collective-permute-done.15.refs_4_
  143.3 5.7 %collective-permute-done.18 = f32[168,512]{1,0:T(8,128)} collective-permute-done((f32[168,512]{1,0:T(8,128)}, f32[168,512]{1,0:T(8,128)}, u32[]{:S(2)}, u32[]{:S(2)}) %collective-permute-start.18) | collective-permute-done | bytes 344096 | tf_op jit(solution)/shard_map/ppermute | solution.py:221
  152.9 5.7 %collective-permute-done.20 = f32[168,512]{1,0:T(8,128)S(1)} collective-permute-done((f32[168,512]{1,0:T(8,128)S(1)}, f32[168,512]{1,0:T(8,128)S(1)}, u32[]{:S(2)}, u32[]{:S(2)}) %collective-permute-start.20) | collective-permute-done | bytes 344096 | tf_op jit(solution)/shard_map/ppermute | solution.py:221
  160.0 5.9 %collective-permute-start.24 = (f32[168,512]{1,0:T(8,128)S(1)}, f32[168,512]{1,0:T(8,128)S(1)}, u32[]{:S(2)}, u32[]{:S(2)}) collective-permute-start(f32[168,512]{1,0:T(8,128)S(1)} %get-tuple-element.476), channel_id=1, source_target_pairs={{0,8},{8,0},{16,24},{24,16},{1,9},{9,1},{17,25},{25,17},{2,10},{10... | collective-permute-start | bytes 1032200 | tf_op jit(solution)/shard_map/ppermute | solution.py:221
  167.5 3.7 collective-permute-done.24
  171.2 2.8 collective-permute-done.23.refs_6_
  177.0 2.3 collective-permute-start.29
  179.5 4.8 %collective-permute-done.26.refs_7_ = f32[168,512]{1,0:T(8,128)S(1)} collective-permute-done((f32[168,512]{1,0:T(8,128)S(1)}, f32[168,512]{1,0:T(8,128)S(1)}, u32[]{:S(2)}, u32[]{:S(2)}) %collective-permute-start.26) | collective-permute-done | bytes 344096 | tf_op jit(solution)/shard_map/ppermute | solution.py:221
  184.2 3.7 collective-permute-done.28.refs_1_
  187.9 2.9 collective-permute-done.27.refs_5_
  191.9 3.0 collective-permute-start.32
  196.5 7.9 %shard_map.65 = (f32[2,168,512]{2,1,0:T(8,128)S(1)}, f32[168,512]{1,0:T(8,128)S(1)}, f32[168,512]{1,0:T(8,128)S(1)}) custom-call(f32[2,2,640,1280]{3,2,1,0:T(8,128)} %k_ref.15, f32[168,512]{1,0:T(8,128)S(1)} %get-tuple-element.277.refs_0_.refs_4_, f32[168,512]{1,0:T(8,128)S(1)} %copy-done.1, f32[168,512]{1,0:T(8,128)S(1)} %broadcast_select_fusion.10.refs_2_, ...), custom_call_target="tpu_custom_call" | custom-call | flops 5033164800 | bytes 10485760 | tf_op jit(solution)/shard_map/pallas_call | solution.py:103
  207.4 9.5 %collective-permute-done.36 = f32[168,512]{1,0:T(8,128)S(1)} collective-permute-done((f32[168,512]{1,0:T(8,128)S(1)}, f32[168,512]{1,0:T(8,128)S(1)}, u32[]{:S(2)}, u32[]{:S(2)}) %collective-permute-start.36) | collective-permute-done | bytes 344096 | tf_op jit(solution)/shard_map/ppermute | solution.py:236
  220.3 6.5 %collective-permute-done.40.refs_6_ = f32[168,512]{1,0:T(8,128)S(1)} collective-permute-done((f32[168,512]{1,0:T(8,128)S(1)}, f32[168,512]{1,0:T(8,128)S(1)}, u32[]{:S(2)}, u32[]{:S(2)}) %collective-permute-start.40) | collective-permute-done | bytes 344096 | tf_op jit(solution)/shard_map/ppermute | solution.py:221
  228.7 5.1 %collective-permute-done.41 = f32[168,512]{1,0:T(8,128)S(1)} collective-permute-done((f32[168,512]{1,0:T(8,128)S(1)}, f32[168,512]{1,0:T(8,128)S(1)}, u32[]{:S(2)}, u32[]{:S(2)}) %collective-permute-start.41) | collective-permute-done | bytes 344096 | tf_op jit(solution)/shard_map/ppermute | solution.py:236
  235.7 8.9 %shard_map.68 = (f32[168,512]{1,0:T(8,128)S(1)}, f32[168,512]{1,0:T(8,128)S(1)}, f32[168,512]{1,0:T(8,128)S(1)}, f32[168,512]{1,0:T(8,128)S(1)}, f32[168,512]{1,...) custom-call(f32[2,2,640,1280]{3,2,1,0:T(8,128)} %k_ref.15, ...), custom_call_target="tpu_custom_call" | custom-call | flops 5033164800 | bytes 10485760 | tf_op jit(solution)/shard_map/pallas_call | solution.py:103
  247.0 7.9 %shard_map.69 = (f32[2,168,512]{2,1,0:T(8,128)S(1)}, f32[168,512]{1,0:T(8,128)S(1)}, f32[168,512]{1,0:T(8,128)S(1)}) custom-call(f32[2,2,640,1280]{3,2,1,0:T(8,128)} %k_ref.15, f32[168,512]{1,0:T(8,128)S(1)} %get-tuple-element.318.refs_0_.refs_4_.refs_7_, f32[168,512]{1,0:T(8,128)S(1)} %collective-permute-done.32.refs_1_, ...), custom_call_target="tpu_custom_call" | custom-call | flops 5033164800 | bytes 10485760 | tf_op jit(solution)/shard_map/pallas_call | solution.py:103
  255.9 2.7 collective-permute-start.48
  261.9 4.7 %collective-permute-done.48 = f32[168,512]{1,0:T(8,128)S(1)} collective-permute-done((f32[168,512]{1,0:T(8,128)S(1)}, f32[168,512]{1,0:T(8,128)S(1)}, u32[]{:S(2)}, u32[]{:S(2)}) %collective-permute-start.48) | collective-permute-done | bytes 344096 | tf_op jit(solution)/shard_map/ppermute | solution.py:235
  266.6 2.3 collective-permute-done.47
  271.0 3.1 collective-permute-start.51
  276.1 4.6 %collective-permute-done.51 = f32[168,512]{1,0:T(8,128)S(1)} collective-permute-done((f32[168,512]{1,0:T(8,128)S(1)}, f32[168,512]{1,0:T(8,128)S(1)}, u32[]{:S(2)}, u32[]{:S(2)}) %collective-permute-start.51) | collective-permute-done | bytes 344096 | tf_op jit(solution)/shard_map/ppermute | solution.py:235
  280.7 4.4 collective-permute-done.53.refs_1_
  285.9 2.4 collective-permute-start.56
  289.0 8.9 %shard_map.71 = (f32[168,512]{1,0:T(8,128)S(1)}, f32[168,512]{1,0:T(8,128)S(1)}, f32[168,512]{1,0:T(8,128)S(1)}, f32[168,512]{1,0:T(8,128)S(1)}, f32[168,512]{1,...) custom-call(f32[2,2,640,1280]{3,2,1,0:T(8,128)} %k_ref.15, ...), custom_call_target="tpu_custom_call" | custom-call | flops 5033164800 | bytes 10485760 | tf_op jit(solution)/shard_map/pallas_call | solution.py:103
  299.3 3.0 collective-permute-start.60
  304.4 6.9 %collective-permute-done.60.refs_1_ = f32[168,512]{1,0:T(8,128)S(1)} collective-permute-done((f32[168,512]{1,0:T(8,128)S(1)}, f32[168,512]{1,0:T(8,128)S(1)}, u32[]{:S(2)}, u32[]{:S(2)}) %collective-permute-start.60) | collective-permute-done | bytes 344096 | tf_op jit(solution)/shard_map/ppermute | solution.py:221
  313.3 5.2 %collective-permute-done.62 = f32[168,512]{1,0:T(8,128)S(1)} collective-permute-done((f32[168,512]{1,0:T(8,128)S(1)}, f32[168,512]{1,0:T(8,128)S(1)}, u32[]{:S(2)}, u32[]{:S(2)}) %collective-permute-start.62) | collective-permute-done | bytes 344096 | tf_op jit(solution)/shard_map/ppermute | solution.py:221
  321.0 5.5 %collective-permute-done.64 = f32[168,512]{1,0:T(8,128)S(1)} collective-permute-done((f32[168,512]{1,0:T(8,128)S(1)}, f32[168,512]{1,0:T(8,128)S(1)}, u32[]{:S(2)}, u32[]{:S(2)}) %collective-permute-start.64) | collective-permute-done | bytes 344096 | tf_op jit(solution)/shard_map/ppermute | solution.py:221
  327.9 6.7 %collective-permute-start.68 = (f32[168,512]{1,0:T(8,128)S(1)}, f32[168,512]{1,0:T(8,128)S(1)}, u32[]{:S(2)}, u32[]{:S(2)}) collective-permute-start(f32[168,512]{1,0:T(8,128)S(1)} %get-tuple-element.472), channel_id=1, source_target_pairs={{0,8},{8,0},{16,24},{24,16},{1,9},{9,1},{17,25},{25,17},{2,10},{10... | collective-permute-start | bytes 1032200 | tf_op jit(solution)/shard_map/ppermute | solution.py:221
  334.9 4.9 %collective-permute-done.68 = f32[168,512]{1,0:T(8,128)S(1)} collective-permute-done((f32[168,512]{1,0:T(8,128)S(1)}, f32[168,512]{1,0:T(8,128)S(1)}, u32[]{:S(2)}, u32[]{:S(2)}) %collective-permute-start.68) | collective-permute-done | bytes 344096 | tf_op jit(solution)/shard_map/ppermute | solution.py:221
  339.8 2.7 collective-permute-done.67.refs_6_
  347.8 5.1 %collective-permute-done.70.refs_7_ = f32[168,512]{1,0:T(8,128)S(1)} collective-permute-done((f32[168,512]{1,0:T(8,128)S(1)}, f32[168,512]{1,0:T(8,128)S(1)}, u32[]{:S(2)}, u32[]{:S(2)}) %collective-permute-start.70) | collective-permute-done | bytes 344096 | tf_op jit(solution)/shard_map/ppermute | solution.py:221
  352.9 3.7 collective-permute-done.72.refs_1_
  356.6 2.2 collective-permute-done.71.refs_5_
  359.9 3.3 collective-permute-start.76
  363.5 7.9 %shard_map.73 = (f32[2,168,512]{2,1,0:T(8,128)S(1)}, f32[168,512]{1,0:T(8,128)S(1)}, f32[168,512]{1,0:T(8,128)S(1)}) custom-call(f32[2,2,640,1280]{3,2,1,0:T(8,128)} %k_ref.15, f32[168,512]{1,0:T(8,128)S(1)} %get-tuple-element.392.refs_0_.refs_1_, f32[168,512]{1,0:T(8,128)S(1)} %collective-permute-done.60.refs_1_, ...), custom_call_target="tpu_custom_call" | custom-call | flops 5033164800 | bytes 10485760 | tf_op jit(solution)/shard_map/pallas_call | solution.py:103
  375.3 8.6 %collective-permute-done.80 = f32[168,512]{1,0:T(8,128)S(1)} collective-permute-done((f32[168,512]{1,0:T(8,128)S(1)}, f32[168,512]{1,0:T(8,128)S(1)}, u32[]{:S(2)}, u32[]{:S(2)}) %collective-permute-start.80) | collective-permute-done | bytes 344096 | tf_op jit(solution)/shard_map/ppermute | solution.py:236
  388.8 4.9 %collective-permute-done.83.refs_6_ = f32[168,512]{1,0:T(8,128)S(1)} collective-permute-done((f32[168,512]{1,0:T(8,128)S(1)}, f32[168,512]{1,0:T(8,128)S(1)}, u32[]{:S(2)}, u32[]{:S(2)}) %collective-permute-start.83) | collective-permute-done | bytes 344096 | tf_op jit(solution)/shard_map/ppermute | solution.py:221
  393.7 5.5 %collective-permute-done.84 = f32[168,512]{1,0:T(8,128)S(1)} collective-permute-done((f32[168,512]{1,0:T(8,128)S(1)}, f32[168,512]{1,0:T(8,128)S(1)}, u32[]{:S(2)}, u32[]{:S(2)}) %collective-permute-start.84) | collective-permute-done | bytes 344096 | tf_op jit(solution)/shard_map/ppermute | solution.py:236
  403.8 3.8 collective-permute-done.86.refs_7_
  409.2 7.9 %shard_map.76 = (f32[2,168,512]{2,1,0:T(8,128)S(1)}, f32[168,512]{1,0:T(8,128)S(1)}, f32[168,512]{1,0:T(8,128)S(1)}) custom-call(f32[2,2,640,1280]{3,2,1,0:T(8,128)} %k_ref.15, f32[168,512]{1,0:T(8,128)S(1)} %get-tuple-element.435.refs_0_.refs_8_, f32[168,512]{1,0:T(8,128)S(1)} %collective-permute-done.76.refs_1_, ...), custom_call_target="tpu_custom_call" | custom-call | flops 5033164800 | bytes 10485760 | tf_op jit(solution)/shard_map/pallas_call | solution.py:103
  417.2 2.1 collective-permute-done.90
  421.3 3.3 collective-permute-done.89
  424.6 5.0 %collective-permute-done.91.refs_2_ = f32[168,512]{1,0:T(8,128)S(1)} collective-permute-done((f32[168,512]{1,0:T(8,128)S(1)}, f32[168,512]{1,0:T(8,128)S(1)}, u32[]{:S(2)}, u32[]{:S(2)}) %collective-permute-start.91) | collective-permute-done | bytes 344096 | tf_op jit(solution)/shard_map/ppermute | solution.py:221
  431.6 3.9 collective-permute-done.92
  439.5 3.3 collective-permute-done.95
  442.7 3.6 collective-permute-done.96
  449.3 2.5 collective-permute-done.97
  (242 shorter events, 103.1 us)
Async XLA Ops:
  37.6 10.5 %collective-permute-start = (f32[168,512]{1,0:T(8,128)S(1)}, f32[168,512]{1,0:T(8,128)S(1)}, u32[]{:S(2)}, u32[]{:S(2)}) collective-permute-start(f32[168,512]{1,0:T(8,128)S(1)} %shard_map.60.refs_0_.refs_3_), channel_id=1, source_target_pairs={{0,2},{2,0},{1,3},{3,1},{4,6},{6,4},{5,7},{7,5},{8,10},{10,8},{9,1... | collective-permute-start | bytes 1032200 | tf_op jit(solution)/shard_map/ppermute | solution.py:221
  58.7 10.2 %collective-permute-start.3 = (f32[168,512]{1,0:T(8,128)S(1)}, f32[168,512]{1,0:T(8,128)S(1)}, u32[]{:S(2)}, u32[]{:S(2)}) collective-permute-start(f32[168,512]{1,0:T(8,128)S(1)} %get-tuple-element.240), channel_id=1, source_target_pairs={{0,4},{4,0},{1,5},{5,1},{2,6},{6,2},{3,7},{7,3},{8,12},{12,8},{9,1... | collective-permute-start | bytes 1032200 | tf_op jit(solution)/shard_map/ppermute | solution.py:221
  59.4 9.8 %collective-permute-start.4 = (f32[168,512]{1,0:T(8,128)S(1)}, f32[168,512]{1,0:T(8,128)S(1)}, u32[]{:S(2)}, u32[]{:S(2)}) collective-permute-start(f32[168,512]{1,0:T(8,128)S(1)} %get-tuple-element.241), channel_id=1, source_target_pairs={{0,8},{8,0},{16,24},{24,16},{1,9},{9,1},{17,25},{25,17},{2,10},{10... | collective-permute-start | bytes 1032200 | tf_op jit(solution)/shard_map/ppermute | solution.py:221
  70.0 21.8 %all-to-all-start.1 = ((f32[8,40,512]{2,1,0:T(8,128)}), f32[8,40,512]{2,1,0:T(8,128)S(1)}, u32[]{:S(2)}, u32[]{:S(2)}) async-start(f32[8,40,512]{2,1,0:T(8,128)} %bitcast.6), calls=%async_computation.1 | async-start | bytes 1310720 | tf_op jit(solution)/shard_map/all_to_all | solution.py:208
  74.6 16.5 %collective-permute-start.6 = (f32[168,512]{1,0:T(8,128)S(1)}, f32[168,512]{1,0:T(8,128)S(1)}, u32[]{:S(2)}, u32[]{:S(2)}) collective-permute-start(f32[168,512]{1,0:T(8,128)S(1)} %add.163), channel_id=1, source_target_pairs={{0,8},{24,16},{1,9},{25,17},{2,10},{26,18},{3,11},{27,19},{4,12},{... | collective-permute-start | bytes 1032200 | tf_op jit(solution)/shard_map/ppermute | solution.py:235
  78.4 13.4 %collective-permute-start.5 = (f32[168,512]{1,0:T(8,128)S(1)}, f32[168,512]{1,0:T(8,128)}, u32[]{:S(2)}, u32[]{:S(2)}) collective-permute-start(f32[168,512]{1,0:T(8,128)S(1)} %get-tuple-element.246), channel_id=1, source_target_pairs={{0,4},{4,0},{1,5},{5,1},{2,6},{6,2},{3,7},{7,3},{8,12},{12,8},{9,1... | collective-permute-start | bytes 1032200 | tf_op jit(solution)/shard_map/ppermute | solution.py:221
  92.6 11.8 %collective-permute-start.10 = (f32[168,512]{1,0:T(8,128)S(1)}, f32[168,512]{1,0:T(8,128)S(1)}, u32[]{:S(2)}, u32[]{:S(2)}) collective-permute-start(f32[168,512]{1,0:T(8,128)S(1)} %shard_map.62.refs_0_.refs_3_), channel_id=1, source_target_pairs={{0,1},{1,0},{2,3},{3,2},{4,5},{5,4},{6,7},{7,6},{8,9},{9,8},{10,11... | collective-permute-start | bytes 1032200 | tf_op jit(solution)/shard_map/ppermute | solution.py:221
  92.6 11.7 %collective-permute-start.9 = (f32[168,512]{1,0:T(8,128)S(1)}, f32[168,512]{1,0:T(8,128)S(1)}, u32[]{:S(2)}, u32[]{:S(2)}) collective-permute-start(f32[168,512]{1,0:T(8,128)S(1)} %shard_map.62.refs_0_.refs_3_), channel_id=1, source_target_pairs={{0,2},{2,0},{1,3},{3,1},{4,6},{6,4},{5,7},{7,5},{8,10},{10,8},{9,1... | collective-permute-start | bytes 1032200 | tf_op jit(solution)/shard_map/ppermute | solution.py:221
  94.3 10.1 %collective-permute-start.8 = (f32[168,512]{1,0:T(8,128)S(1)}, f32[168,512]{1,0:T(8,128)S(1)}, u32[]{:S(2)}, u32[]{:S(2)}) collective-permute-start(f32[168,512]{1,0:T(8,128)S(1)} %add.166), channel_id=1, source_target_pairs={{8,16},{16,8},{9,17},{17,9},{10,18},{18,10},{11,19},{19,11},{12,20... | collective-permute-start | bytes 1032200 | tf_op jit(solution)/shard_map/ppermute | solution.py:234
  96.1 15.6 %collective-permute-start.7 = (f32[168,512]{1,0:T(8,128)S(1)}, f32[168,512]{1,0:T(8,128)S(1)}, u32[]{:S(2)}, u32[]{:S(2)}) collective-permute-start(f32[168,512]{1,0:T(8,128)S(1)} %add.165), channel_id=1, source_target_pairs={{0,8},{24,16},{1,9},{25,17},{2,10},{26,18},{3,11},{27,19},{4,12},{... | collective-permute-start | bytes 1032200 | tf_op jit(solution)/shard_map/ppermute | solution.py:235
  111.7 16.3 %collective-permute-start.13 = (f32[168,512]{1,0:T(8,128)S(1)}, f32[168,512]{1,0:T(8,128)S(1)}, u32[]{:S(2)}, u32[]{:S(2)}) collective-permute-start(f32[168,512]{1,0:T(8,128)S(1)} %add.168), channel_id=1, source_target_pairs={{8,16},{16,8},{9,17},{17,9},{10,18},{18,10},{11,19},{19,11},{12,20... | collective-permute-start | bytes 1032200 | tf_op jit(solution)/shard_map/ppermute | solution.py:234
  112.6 15.4 %collective-permute-start.12 = (f32[168,512]{1,0:T(8,128)S(1)}, f32[168,512]{1,0:T(8,128)S(1)}, u32[]{:S(2)}, u32[]{:S(2)}) collective-permute-start(f32[168,512]{1,0:T(8,128)S(1)} %add.167), channel_id=1, source_target_pairs={{0,8},{8,0},{16,24},{24,16},{1,9},{9,1},{17,25},{25,17},{2,10},{10... | collective-permute-start | bytes 1032200 | tf_op jit(solution)/shard_map/ppermute | solution.py:221
  116.7 11.3 %collective-permute-start.11 = (f32[168,512]{1,0:T(8,128)S(1)}, f32[168,512]{1,0:T(8,128)S(1)}, u32[]{:S(2)}, u32[]{:S(2)}) collective-permute-start(f32[168,512]{1,0:T(8,128)S(1)} %copy-done.6), channel_id=1, source_target_pairs={{0,4},{4,0},{1,5},{5,1},{2,6},{6,2},{3,7},{7,3},{8,12},{12,8},{9,1... | collective-permute-start | bytes 1032200 | tf_op jit(solution)/shard_map/ppermute | solution.py:221
  129.8 11.3 %collective-permute-start.16 = (f32[168,512]{1,0:T(8,128)S(1)}, f32[168,512]{1,0:T(8,128)S(1)}, u32[]{:S(2)}, u32[]{:S(2)}) collective-permute-start(f32[168,512]{1,0:T(8,128)S(1)} %get-tuple-element.277.refs_0_.refs_4_), channel_id=1, source_target_pairs={{0,8},{8,0},{16,24},{24,16},{1,9},{9,1},{17,25},{25,17},{2,10},{10... | collective-permute-start | bytes 1032200 | tf_op jit(solution)/shard_map/ppermute | solution.py:221
  132.2 11.1 %collective-permute-start.15 = (f32[168,512]{1,0:T(8,128)S(1)}, f32[168,512]{1,0:T(8,128)}, u32[]{:S(2)}, u32[]{:S(2)}) collective-permute-start(f32[168,512]{1,0:T(8,128)S(1)} %get-tuple-element.277.refs_0_.refs_4_), channel_id=1, source_target_pairs={{0,4},{4,0},{1,5},{5,1},{2,6},{6,2},{3,7},{7,3},{8,12},{12,8},{9,1... | collective-permute-start | bytes 1032200 | tf_op jit(solution)/shard_map/ppermute | solution.py:221
  132.7 16.3 %collective-permute-start.18 = (f32[168,512]{1,0:T(8,128)}, f32[168,512]{1,0:T(8,128)}, u32[]{:S(2)}, u32[]{:S(2)}) collective-permute-start(f32[168,512]{1,0:T(8,128)} %get-tuple-element.278), channel_id=1, source_target_pairs={{0,4},{4,0},{1,5},{5,1},{2,6},{6,2},{3,7},{7,3},{8,12},{12,8},{9,1... | collective-permute-start | bytes 1032200 | tf_op jit(solution)/shard_map/ppermute | solution.py:221
  134.2 14.8 %collective-permute-start.19 = (f32[168,512]{1,0:T(8,128)}, f32[168,512]{1,0:T(8,128)}, u32[]{:S(2)}, u32[]{:S(2)}) collective-permute-start(f32[168,512]{1,0:T(8,128)} %get-tuple-element.279), channel_id=1, source_target_pairs={{0,8},{8,0},{16,24},{24,16},{1,9},{9,1},{17,25},{25,17},{2,10},{10... | collective-permute-start | bytes 1032200 | tf_op jit(solution)/shard_map/ppermute | solution.py:221
  150.1 8.5 %collective-permute-start.20 = (f32[168,512]{1,0:T(8,128)S(1)}, f32[168,512]{1,0:T(8,128)S(1)}, u32[]{:S(2)}, u32[]{:S(2)}) collective-permute-start(f32[168,512]{1,0:T(8,128)S(1)} %get-tuple-element.478), channel_id=1, source_target_pairs={{0,8},{8,0},{16,24},{24,16},{1,9},{9,1},{17,25},{25,17},{2,10},{10... | collective-permute-start | bytes 1032200 | tf_op jit(solution)/shard_map/ppermute | solution.py:221
  150.7 8.5 %collective-permute-start.22 = (f32[168,512]{1,0:T(8,128)S(1)}, f32[168,512]{1,0:T(8,128)S(1)}, u32[]{:S(2)}, u32[]{:S(2)}) collective-permute-start(f32[168,512]{1,0:T(8,128)S(1)} %copy-done.3), channel_id=1, source_target_pairs={{0,4},{4,0},{1,5},{5,1},{2,6},{6,2},{3,7},{7,3},{8,12},{12,8},{9,1... | collective-permute-start | bytes 1032200 | tf_op jit(solution)/shard_map/ppermute | solution.py:221
  160.0 11.1 %collective-permute-start.24 = (f32[168,512]{1,0:T(8,128)S(1)}, f32[168,512]{1,0:T(8,128)S(1)}, u32[]{:S(2)}, u32[]{:S(2)}) collective-permute-start(f32[168,512]{1,0:T(8,128)S(1)} %get-tuple-element.476), channel_id=1, source_target_pairs={{0,8},{8,0},{16,24},{24,16},{1,9},{9,1},{17,25},{25,17},{2,10},{10... | collective-permute-start | bytes 1032200 | tf_op jit(solution)/shard_map/ppermute | solution.py:221
  174.9 9.4 %collective-permute-start.26 = (f32[168,512]{1,0:T(8,128)S(1)}, f32[168,512]{1,0:T(8,128)S(1)}, u32[]{:S(2)}, u32[]{:S(2)}) collective-permute-start(f32[168,512]{1,0:T(8,128)S(1)} %broadcast_select_fusion.8.refs_3_), channel_id=1, source_target_pairs={{0,4},{4,0},{1,5},{5,1},{2,6},{6,2},{3,7},{7,3},{8,12},{12,8},{9,1... | collective-permute-start | bytes 1032200 | tf_op jit(solution)/shard_map/ppermute | solution.py:221
  176.5 11.5 %collective-permute-start.28 = (f32[168,512]{1,0:T(8,128)S(1)}, f32[168,512]{1,0:T(8,128)S(1)}, u32[]{:S(2)}, u32[]{:S(2)}) collective-permute-start(f32[168,512]{1,0:T(8,128)S(1)} %add.170), channel_id=1, source_target_pairs={{0,4},{4,0},{1,5},{5,1},{2,6},{6,2},{3,7},{7,3},{8,12},{12,8},{9,1... | collective-permute-start | bytes 1032200 | tf_op jit(solution)/shard_map/ppermute | solution.py:221
  177.0 10.9 %collective-permute-start.29 = (f32[168,512]{1,0:T(8,128)S(1)}, f32[168,512]{1,0:T(8,128)S(1)}, u32[]{:S(2)}, u32[]{:S(2)}) collective-permute-start(f32[168,512]{1,0:T(8,128)S(1)} %add.173), channel_id=1, source_target_pairs={{0,8},{8,0},{16,24},{24,16},{1,9},{9,1},{17,25},{25,17},{2,10},{10... | collective-permute-start | bytes 1032200 | tf_op jit(solution)/shard_map/ppermute | solution.py:221
  179.4 11.5 %collective-permute-start.27 = (f32[168,512]{1,0:T(8,128)}, f32[168,512]{1,0:T(8,128)S(1)}, u32[]{:S(2)}, u32[]{:S(2)}) collective-permute-start(f32[168,512]{1,0:T(8,128)} %collective-permute-done.15.refs_4_), channel_id=1, source_target_pairs={{0,8},{8,0},{16,24},{24,16},{1,9},{9,1},{17,25},{25,17},{2,10},{10... | collective-permute-start | bytes 1032200 | tf_op jit(solution)/shard_map/ppermute | solution.py:221
  191.2 13.2 %collective-permute-start.33 = (f32[168,512]{1,0:T(8,128)S(1)}, f32[168,512]{1,0:T(8,128)S(1)}, u32[]{:S(2)}, u32[]{:S(2)}) collective-permute-start(f32[168,512]{1,0:T(8,128)S(1)} %get-tuple-element.318.refs_0_.refs_4_.refs_7_), channel_id=1, source_target_pairs={{8,16},{16,8},{9,17},{17,9},{10,18},{18,10},{11,19},{19,11},{12,20... | collective-permute-start | bytes 1032200 | tf_op jit(solution)/shard_map/ppermute | solution.py:234
  191.9 12.5 %collective-permute-start.32 = (f32[168,512]{1,0:T(8,128)S(1)}, f32[168,512]{1,0:T(8,128)S(1)}, u32[]{:S(2)}, u32[]{:S(2)}) collective-permute-start(f32[168,512]{1,0:T(8,128)S(1)} %get-tuple-element.318.refs_0_.refs_4_.refs_7_), channel_id=1, source_target_pairs={{0,8},{8,0},{16,24},{24,16},{1,9},{9,1},{17,25},{25,17},{2,10},{10... | collective-permute-start | bytes 1032200 | tf_op jit(solution)/shard_map/ppermute | solution.py:221
  195.0 9.5 %collective-permute-start.31 = (f32[168,512]{1,0:T(8,128)S(1)}, f32[168,512]{1,0:T(8,128)S(1)}, u32[]{:S(2)}, u32[]{:S(2)}) collective-permute-start(f32[168,512]{1,0:T(8,128)S(1)} %get-tuple-element.318.refs_0_.refs_4_.refs_7_), channel_id=1, source_target_pairs={{0,4},{4,0},{1,5},{5,1},{2,6},{6,2},{3,7},{7,3},{8,12},{12,8},{9,1... | collective-permute-start | bytes 1032200 | tf_op jit(solution)/shard_map/ppermute | solution.py:221
  204.6 12.3 %collective-permute-start.36 = (f32[168,512]{1,0:T(8,128)S(1)}, f32[168,512]{1,0:T(8,128)S(1)}, u32[]{:S(2)}, u32[]{:S(2)}) collective-permute-start(f32[168,512]{1,0:T(8,128)S(1)} %collective-permute-done.33), channel_id=1, source_target_pairs={{8,0},{16,24},{9,1},{17,25},{10,2},{18,26},{11,3},{19,27},{12,4},{... | collective-permute-start | bytes 1032200 | tf_op jit(solution)/shard_map/ppermute | solution.py:236
  205.9 11.0 %collective-permute-start.37 = (f32[168,512]{1,0:T(8,128)S(1)}, f32[168,512]{1,0:T(8,128)S(1)}, u32[]{:S(2)}, u32[]{:S(2)}) collective-permute-start(f32[168,512]{1,0:T(8,128)S(1)} %collective-permute-done.32.refs_1_), channel_id=1, source_target_pairs={{8,16},{16,8},{9,17},{17,9},{10,18},{18,10},{11,19},{19,11},{12,20... | collective-permute-start | bytes 1032200 | tf_op jit(solution)/shard_map/ppermute | solution.py:234
  206.7 10.4 %collective-permute-start.35 = (f32[168,512]{1,0:T(8,128)S(1)}, f32[168,512]{1,0:T(8,128)S(1)}, u32[]{:S(2)}, u32[]{:S(2)}) collective-permute-start(f32[168,512]{1,0:T(8,128)S(1)} %fusion.4), channel_id=1, source_target_pairs={{0,2},{2,0},{1,3},{3,1},{4,6},{6,4},{5,7},{7,5},{8,10},{10,8},{9,1... | collective-permute-start | bytes 1032200 | tf_op jit(solution)/shard_map/ppermute | solution.py:221
  217.2 9.6 %collective-permute-start.40 = (f32[168,512]{1,0:T(8,128)S(1)}, f32[168,512]{1,0:T(8,128)S(1)}, u32[]{:S(2)}, u32[]{:S(2)}) collective-permute-start(f32[168,512]{1,0:T(8,128)S(1)} %broadcast_select_fusion.7.refs_2_), channel_id=1, source_target_pairs={{0,4},{4,0},{1,5},{5,1},{2,6},{6,2},{3,7},{7,3},{8,12},{12,8},{9,1... | collective-permute-start | bytes 1032200 | tf_op jit(solution)/shard_map/ppermute | solution.py:221
  218.1 8.7 %collective-permute-start.39 = (f32[168,512]{1,0:T(8,128)S(1)}, f32[168,512]{1,0:T(8,128)S(1)}, u32[]{:S(2)}, u32[]{:S(2)}) collective-permute-start(f32[168,512]{1,0:T(8,128)S(1)} %get-tuple-element.327.refs_0_.refs_3_), channel_id=1, source_target_pairs={{0,1},{1,0},{2,3},{3,2},{4,5},{5,4},{6,7},{7,6},{8,9},{9,8},{10,11... | collective-permute-start | bytes 1032200 | tf_op jit(solution)/shard_map/ppermute | solution.py:221
  218.2 10.5 %collective-permute-start.38 = (f32[168,512]{1,0:T(8,128)S(1)}, f32[168,512]{1,0:T(8,128)S(1)}, u32[]{:S(2)}, u32[]{:S(2)}) collective-permute-start(f32[168,512]{1,0:T(8,128)S(1)} %get-tuple-element.327.refs_0_.refs_3_), channel_id=1, source_target_pairs={{0,2},{2,0},{1,3},{3,1},{4,6},{6,4},{5,7},{7,5},{8,10},{10,8},{9,1... | collective-permute-start | bytes 1032200 | tf_op jit(solution)/shard_map/ppermute | solution.py:221
  218.8 15.0 %collective-permute-start.41 = (f32[168,512]{1,0:T(8,128)S(1)}, f32[168,512]{1,0:T(8,128)S(1)}, u32[]{:S(2)}, u32[]{:S(2)}) collective-permute-start(f32[168,512]{1,0:T(8,128)S(1)} %collective-permute-done.37), channel_id=1, source_target_pairs={{8,0},{16,24},{9,1},{17,25},{10,2},{18,26},{11,3},{19,27},{12,4},{... | collective-permute-start | bytes 1032200 | tf_op jit(solution)/shard_map/ppermute | solution.py:236
  233.9 10.8 %collective-permute-start.43 = (f32[168,512]{1,0:T(8,128)S(1)}, f32[168,512]{1,0:T(8,128)S(1)}, u32[]{:S(2)}, u32[]{:S(2)}) collective-permute-start(f32[168,512]{1,0:T(8,128)S(1)} %broadcast_select_fusion.6.refs_3_), channel_id=1, source_target_pairs={{0,4},{4,0},{1,5},{5,1},{2,6},{6,2},{3,7},{7,3},{8,12},{12,8},{9,1... | collective-permute-start | bytes 1032200 | tf_op jit(solution)/shard_map/ppermute | solution.py:221
  235.4 10.2 %collective-permute-start.44 = (f32[168,512]{1,0:T(8,128)S(1)}, f32[168,512]{1,0:T(8,128)S(1)}, u32[]{:S(2)}, u32[]{:S(2)}) collective-permute-start(f32[168,512]{1,0:T(8,128)S(1)} %collective-permute-done.31.refs_4_), channel_id=1, source_target_pairs={{0,8},{8,0},{16,24},{24,16},{1,9},{9,1},{17,25},{25,17},{2,10},{10... | collective-permute-start | bytes 1032200 | tf_op jit(solution)/shard_map/ppermute | solution.py:221
  245.6 9.4 %collective-permute-start.45 = (f32[168,512]{1,0:T(8,128)S(1)}, f32[168,512]{1,0:T(8,128)S(1)}, u32[]{:S(2)}, u32[]{:S(2)}) collective-permute-start(f32[168,512]{1,0:T(8,128)S(1)} %get-tuple-element.345), channel_id=1, source_target_pairs={{0,4},{4,0},{1,5},{5,1},{2,6},{6,2},{3,7},{7,3},{8,12},{12,8},{9,1... | collective-permute-start | bytes 1032200 | tf_op jit(solution)/shard_map/ppermute | solution.py:221
  246.1 9.7 %collective-permute-start.46 = (f32[168,512]{1,0:T(8,128)S(1)}, f32[168,512]{1,0:T(8,128)S(1)}, u32[]{:S(2)}, u32[]{:S(2)}) collective-permute-start(f32[168,512]{1,0:T(8,128)S(1)} %get-tuple-element.346), channel_id=1, source_target_pairs={{0,8},{8,0},{16,24},{24,16},{1,9},{9,1},{17,25},{25,17},{2,10},{10... | collective-permute-start | bytes 1032200 | tf_op jit(solution)/shard_map/ppermute | solution.py:221
  255.9 10.7 %collective-permute-start.48 = (f32[168,512]{1,0:T(8,128)S(1)}, f32[168,512]{1,0:T(8,128)S(1)}, u32[]{:S(2)}, u32[]{:S(2)}) collective-permute-start(f32[168,512]{1,0:T(8,128)S(1)} %add.176), channel_id=1, source_target_pairs={{0,8},{24,16},{1,9},{25,17},{2,10},{26,18},{3,11},{27,19},{4,12},{... | collective-permute-start | bytes 1032200 | tf_op jit(solution)/shard_map/ppermute | solution.py:235
  258.6 10.3 %collective-permute-start.47 = (f32[168,512]{1,0:T(8,128)S(1)}, f32[168,512]{1,0:T(8,128)S(1)}, u32[]{:S(2)}, u32[]{:S(2)}) collective-permute-start(f32[168,512]{1,0:T(8,128)S(1)} %get-tuple-element.356), channel_id=1, source_target_pairs={{0,4},{4,0},{1,5},{5,1},{2,6},{6,2},{3,7},{7,3},{8,12},{12,8},{9,1... | collective-permute-start | bytes 1032200 | tf_op jit(solution)/shard_map/ppermute | solution.py:221
  260.3 10.0 %collective-permute-start.50 = (f32[168,512]{1,0:T(8,128)S(1)}, f32[168,512]{1,0:T(8,128)S(1)}, u32[]{:S(2)}, u32[]{:S(2)}) collective-permute-start(f32[168,512]{1,0:T(8,128)S(1)} %fusion.3), channel_id=1, source_target_pairs={{0,2},{2,0},{1,3},{3,1},{4,6},{6,4},{5,7},{7,5},{8,10},{10,8},{9,1... | collective-permute-start | bytes 1032200 | tf_op jit(solution)/shard_map/ppermute | solution.py:221
  271.0 9.7 %collective-permute-start.51 = (f32[168,512]{1,0:T(8,128)S(1)}, f32[168,512]{1,0:T(8,128)S(1)}, u32[]{:S(2)}, u32[]{:S(2)}) collective-permute-start(f32[168,512]{1,0:T(8,128)S(1)} %add.179), channel_id=1, source_target_pairs={{0,8},{24,16},{1,9},{25,17},{2,10},{26,18},{3,11},{27,19},{4,12},{... | collective-permute-start | bytes 1032200 | tf_op jit(solution)/shard_map/ppermute | solution.py:235
  274.6 10.5 %collective-permute-start.53 = (f32[168,512]{1,0:T(8,128)S(1)}, f32[168,512]{1,0:T(8,128)S(1)}, u32[]{:S(2)}, u32[]{:S(2)}) collective-permute-start(f32[168,512]{1,0:T(8,128)S(1)} %get-tuple-element.372.refs_0_.refs_3_), channel_id=1, source_target_pairs={{0,2},{2,0},{1,3},{3,1},{4,6},{6,4},{5,7},{7,5},{8,10},{10,8},{9,1... | collective-permute-start | bytes 1032200 | tf_op jit(solution)/shard_map/ppermute | solution.py:221
  285.1 12.8 %collective-permute-start.57 = (f32[168,512]{1,0:T(8,128)S(1)}, f32[168,512]{1,0:T(8,128)S(1)}, u32[]{:S(2)}, u32[]{:S(2)}) collective-permute-start(f32[168,512]{1,0:T(8,128)S(1)} %add.182), channel_id=1, source_target_pairs={{8,16},{16,8},{9,17},{17,9},{10,18},{18,10},{11,19},{19,11},{12,20... | collective-permute-start | bytes 1032200 | tf_op jit(solution)/shard_map/ppermute | solution.py:234
  285.9 12.0 %collective-permute-start.56 = (f32[168,512]{1,0:T(8,128)S(1)}, f32[168,512]{1,0:T(8,128)S(1)}, u32[]{:S(2)}, u32[]{:S(2)}) collective-permute-start(f32[168,512]{1,0:T(8,128)S(1)} %add.181), channel_id=1, source_target_pairs={{0,8},{8,0},{16,24},{24,16},{1,9},{9,1},{17,25},{25,17},{2,10},{10... | collective-permute-start | bytes 1032200 | tf_op jit(solution)/shard_map/ppermute | solution.py:221
  288.3 9.9 %collective-permute-start.55 = (f32[168,512]{1,0:T(8,128)S(1)}, f32[168,512]{1,0:T(8,128)S(1)}, u32[]{:S(2)}, u32[]{:S(2)}) collective-permute-start(f32[168,512]{1,0:T(8,128)S(1)} %add.177), channel_id=1, source_target_pairs={{0,4},{4,0},{1,5},{5,1},{2,6},{6,2},{3,7},{7,3},{8,12},{12,8},{9,1... | collective-permute-start | bytes 1032200 | tf_op jit(solution)/shard_map/ppermute | solution.py:221
  299.3 12.0 %collective-permute-start.60 = (f32[168,512]{1,0:T(8,128)S(1)}, f32[168,512]{1,0:T(8,128)S(1)}, u32[]{:S(2)}, u32[]{:S(2)}) collective-permute-start(f32[168,512]{1,0:T(8,128)S(1)} %get-tuple-element.392.refs_0_.refs_1_), channel_id=1, source_target_pairs={{0,8},{8,0},{16,24},{24,16},{1,9},{9,1},{17,25},{25,17},{2,10},{10... | collective-permute-start | bytes 1032200 | tf_op jit(solution)/shard_map/ppermute | solution.py:221
  302.3 11.0 %collective-permute-start.59 = (f32[168,512]{1,0:T(8,128)S(1)}, f32[168,512]{1,0:T(8,128)S(1)}, u32[]{:S(2)}, u32[]{:S(2)}) collective-permute-start(f32[168,512]{1,0:T(8,128)S(1)} %get-tuple-element.392.refs_0_.refs_1_), channel_id=1, source_target_pairs={{0,4},{4,0},{1,5},{5,1},{2,6},{6,2},{3,7},{7,3},{8,12},{12,8},{9,1... | collective-permute-start | bytes 1032200 | tf_op jit(solution)/shard_map/ppermute | solution.py:221
  303.1 15.4 %collective-permute-start.62 = (f32[168,512]{1,0:T(8,128)S(1)}, f32[168,512]{1,0:T(8,128)S(1)}, u32[]{:S(2)}, u32[]{:S(2)}) collective-permute-start(f32[168,512]{1,0:T(8,128)S(1)} %get-tuple-element.394), channel_id=1, source_target_pairs={{0,4},{4,0},{1,5},{5,1},{2,6},{6,2},{3,7},{7,3},{8,12},{12,8},{9,1... | collective-permute-start | bytes 1032200 | tf_op jit(solution)/shard_map/ppermute | solution.py:221
  304.3 14.2 %collective-permute-start.63 = (f32[168,512]{1,0:T(8,128)S(1)}, f32[168,512]{1,0:T(8,128)S(1)}, u32[]{:S(2)}, u32[]{:S(2)}) collective-permute-start(f32[168,512]{1,0:T(8,128)S(1)} %get-tuple-element.395), channel_id=1, source_target_pairs={{0,8},{8,0},{16,24},{24,16},{1,9},{9,1},{17,25},{25,17},{2,10},{10... | collective-permute-start | bytes 1032200 | tf_op jit(solution)/shard_map/ppermute | solution.py:221
  327.9 11.9 %collective-permute-start.68 = (f32[168,512]{1,0:T(8,128)S(1)}, f32[168,512]{1,0:T(8,128)S(1)}, u32[]{:S(2)}, u32[]{:S(2)}) collective-permute-start(f32[168,512]{1,0:T(8,128)S(1)} %get-tuple-element.472), channel_id=1, source_target_pairs={{0,8},{8,0},{16,24},{24,16},{1,9},{9,1},{17,25},{25,17},{2,10},{10... | collective-permute-start | bytes 1032200 | tf_op jit(solution)/shard_map/ppermute | solution.py:221
  343.5 9.4 %collective-permute-start.70 = (f32[168,512]{1,0:T(8,128)S(1)}, f32[168,512]{1,0:T(8,128)S(1)}, u32[]{:S(2)}, u32[]{:S(2)}) collective-permute-start(f32[168,512]{1,0:T(8,128)S(1)} %broadcast_select_fusion.2.refs_3_), channel_id=1, source_target_pairs={{0,4},{4,0},{1,5},{5,1},{2,6},{6,2},{3,7},{7,3},{8,12},{12,8},{9,1... | collective-permute-start | bytes 1032200 | tf_op jit(solution)/shard_map/ppermute | solution.py:221
  343.9 12.7 %collective-permute-start.72 = (f32[168,512]{1,0:T(8,128)S(1)}, f32[168,512]{1,0:T(8,128)S(1)}, u32[]{:S(2)}, u32[]{:S(2)}) collective-permute-start(f32[168,512]{1,0:T(8,128)S(1)} %add.184), channel_id=1, source_target_pairs={{0,4},{4,0},{1,5},{5,1},{2,6},{6,2},{3,7},{7,3},{8,12},{12,8},{9,1... | collective-permute-start | bytes 1032200 | tf_op jit(solution)/shard_map/ppermute | solution.py:221
  345.7 10.9 %collective-permute-start.73 = (f32[168,512]{1,0:T(8,128)S(1)}, f32[168,512]{1,0:T(8,128)S(1)}, u32[]{:S(2)}, u32[]{:S(2)}) collective-permute-start(f32[168,512]{1,0:T(8,128)S(1)} %add.187), channel_id=1, source_target_pairs={{0,8},{8,0},{16,24},{24,16},{1,9},{9,1},{17,25},{25,17},{2,10},{10... | collective-permute-start | bytes 1032200 | tf_op jit(solution)/shard_map/ppermute | solution.py:221
  347.8 11.1 %collective-permute-start.71 = (f32[168,512]{1,0:T(8,128)S(1)}, f32[168,512]{1,0:T(8,128)S(1)}, u32[]{:S(2)}, u32[]{:S(2)}) collective-permute-start(f32[168,512]{1,0:T(8,128)S(1)} %collective-permute-done.59.refs_4_), channel_id=1, source_target_pairs={{0,8},{8,0},{16,24},{24,16},{1,9},{9,1},{17,25},{25,17},{2,10},{10... | collective-permute-start | bytes 1032200 | tf_op jit(solution)/shard_map/ppermute | solution.py:221
  359.2 12.2 %collective-permute-start.77 = (f32[168,512]{1,0:T(8,128)S(1)}, f32[168,512]{1,0:T(8,128)S(1)}, u32[]{:S(2)}, u32[]{:S(2)}) collective-permute-start(f32[168,512]{1,0:T(8,128)S(1)} %get-tuple-element.435.refs_0_.refs_8_), channel_id=1, source_target_pairs={{8,16},{16,8},{9,17},{17,9},{10,18},{18,10},{11,19},{19,11},{12,20... | collective-permute-start | bytes 1032200 | tf_op jit(solution)/shard_map/ppermute | solution.py:234
  359.9 11.5 %collective-permute-start.76 = (f32[168,512]{1,0:T(8,128)S(1)}, f32[168,512]{1,0:T(8,128)S(1)}, u32[]{:S(2)}, u32[]{:S(2)}) collective-permute-start(f32[168,512]{1,0:T(8,128)S(1)} %get-tuple-element.435.refs_0_.refs_8_), channel_id=1, source_target_pairs={{0,8},{8,0},{16,24},{24,16},{1,9},{9,1},{17,25},{25,17},{2,10},{10... | collective-permute-start | bytes 1032200 | tf_op jit(solution)/shard_map/ppermute | solution.py:221
  371.5 12.3 %collective-permute-start.80 = (f32[168,512]{1,0:T(8,128)S(1)}, f32[168,512]{1,0:T(8,128)S(1)}, u32[]{:S(2)}, u32[]{:S(2)}) collective-permute-start(f32[168,512]{1,0:T(8,128)S(1)} %collective-permute-done.77), channel_id=1, source_target_pairs={{8,0},{16,24},{9,1},{17,25},{10,2},{18,26},{11,3},{19,27},{12,4},{... | collective-permute-start | bytes 1032200 | tf_op jit(solution)/shard_map/ppermute | solution.py:236
  372.8 11.0 %collective-permute-start.81 = (f32[168,512]{1,0:T(8,128)S(1)}, f32[168,512]{1,0:T(8,128)S(1)}, u32[]{:S(2)}, u32[]{:S(2)}) collective-permute-start(f32[168,512]{1,0:T(8,128)S(1)} %collective-permute-done.76.refs_1_), channel_id=1, source_target_pairs={{8,16},{16,8},{9,17},{17,9},{10,18},{18,10},{11,19},{19,11},{12,20... | collective-permute-start | bytes 1032200 | tf_op jit(solution)/shard_map/ppermute | solution.py:234
  373.7 10.4 %collective-permute-start.79 = (f32[168,512]{1,0:T(8,128)S(1)}, f32[168,512]{1,0:T(8,128)S(1)}, u32[]{:S(2)}, u32[]{:S(2)}) collective-permute-start(f32[168,512]{1,0:T(8,128)S(1)} %fusion.2), channel_id=1, source_target_pairs={{0,2},{2,0},{1,3},{3,1},{4,6},{6,4},{5,7},{7,5},{8,10},{10,8},{9,1... | collective-permute-start | bytes 1032200 | tf_op jit(solution)/shard_map/ppermute | solution.py:221
  384.2 9.6 %collective-permute-start.83 = (f32[168,512]{1,0:T(8,128)S(1)}, f32[168,512]{1,0:T(8,128)S(1)}, u32[]{:S(2)}, u32[]{:S(2)}) collective-permute-start(f32[168,512]{1,0:T(8,128)S(1)} %broadcast_select_fusion.1.refs_2_), channel_id=1, source_target_pairs={{0,4},{4,0},{1,5},{5,1},{2,6},{6,2},{3,7},{7,3},{8,12},{12,8},{9,1... | collective-permute-start | bytes 1032200 | tf_op jit(solution)/shard_map/ppermute | solution.py:221
  385.9 13.4 %collective-permute-start.84 = (f32[168,512]{1,0:T(8,128)S(1)}, f32[168,512]{1,0:T(8,128)S(1)}, u32[]{:S(2)}, u32[]{:S(2)}) collective-permute-start(f32[168,512]{1,0:T(8,128)S(1)} %collective-permute-done.81), channel_id=1, source_target_pairs={{8,0},{16,24},{9,1},{17,25},{10,2},{18,26},{11,3},{19,27},{12,4},{... | collective-permute-start | bytes 1032200 | tf_op jit(solution)/shard_map/ppermute | solution.py:236
  407.6 9.6 %collective-permute-start.88 = (f32[8,128]{1,0:T(8,128)S(1)}, f32[8,128]{1,0:T(8,128)S(1)}, u32[]{:S(2)}, u32[]{:S(2)}) collective-permute-start(f32[8,128]{1,0:T(8,128)S(1)} %add.191), channel_id=1, source_target_pairs={{0,4},{4,0},{1,5},{5,1},{2,6},{6,2},{3,7},{7,3},{8,12},{12,8},{9,1... | collective-permute-start | bytes 12296 | tf_op jit(solution)/shard_map/ppermute | solution.py:221
  419.4 10.2 %collective-permute-start.91 = (f32[168,512]{1,0:T(8,128)S(1)}, f32[168,512]{1,0:T(8,128)S(1)}, u32[]{:S(2)}, u32[]{:S(2)}) collective-permute-start(f32[168,512]{1,0:T(8,128)S(1)} %fusion.1), channel_id=1, source_target_pairs={{0,2},{2,0},{1,3},{3,1},{4,6},{6,4},{5,7},{7,5},{8,10},{10,8},{9,1... | collective-permute-start | bytes 1032200 | tf_op jit(solution)/shard_map/ppermute | solution.py:221
  (46 other events, 278.6 us)
